TPU v7x, 256 devices: a whole 4x4x8 slice. The times are simulated.
256 devices in a mesh: dp: 8 (over z), expert: 32 (over y, x, core).
Axes of the slice: x: 4, y: 4, z: 8, core: 2. Of those that a mesh axis runs over, the one named last changes fastest.
Arguments:
- activations: bfloat16 [32768, 2048], P(('dp', 'expert')), may hold values from -6 to 6
- expert_ids: int32 [32768, 8], P(('dp', 'expert')), may hold values from 0 to 127, all different within a row; in each aligned block of 128 rows (0 to 127, 128 to 255, ...) at most 12 rows name the same one
- route_gates: float32 [32768, 8], P(('dp', 'expert')), may hold values from 0.2 to 1
- gate_proj: bfloat16 [32, 2048, 768], P('expert'), may hold values from -0.125 to 0.125
- up_proj: bfloat16 [32, 2048, 768], P('expert'), may hold values from -0.125 to 0.125
- down_proj: bfloat16 [32, 2048, 768], P('expert'), may hold values from -0.21875 to 0.21875
- cotangent: bfloat16 [32768, 2048], P(('dp', 'expert')), may hold values from -3 to 3
Outputs:
- layer_out: bfloat16 [32768, 2048], P(('dp', 'expert'))
- grad_input: bfloat16 [32768, 2048], P(('dp', 'expert'))
- grad_gate: bfloat16 [32, 2048, 768], P('expert', 'dp')
- grad_up: bfloat16 [32, 2048, 768], P('expert', 'dp')
- grad_down: bfloat16 [32, 2048, 768], P('expert', 'dp')
Inputs may be any that keep to these rules, and one draw needn't show every extreme that they name: `expert_ids`: each row names 8 different experts. Within the 128 rows of one device no expert is named by more than 12 rows; in some devices' rows an expert is named by exactly 12.
All inputs are finite; a program needn't handle non-finite values.
Results may differ from a plain program's by a relative error of at most 0.017.
Values may be sent and summed in bfloat16 or wider, within the bound.
A program may use at most 128 MiB of HBM per device.

v0:
```python
import jax
import jax.numpy as jnp
from jax import lax
from jax.sharding import PartitionSpec as P

CAP = 12


def contract_rows(left_side, right_side):
    return lax.dot_general(
        left_side, right_side, (((0,), (0,)), ((), ())), preferred_element_type=jnp.float32
    )


def contract_cols(left_side, right_side):
    return lax.dot_general(
        left_side, right_side, (((1,), (1,)), ((), ())), preferred_element_type=jnp.float32
    )


def run_rows(step, pieces):
    return tuple(step(*pieces))


def shards(activations, expert_ids, route_gates, gate_proj, up_proj, down_proj, cotangent):
    window_size = lax.axis_size("expert")
    token_count = activations.shape[0]
    model_width = activations.shape[1]
    gate_matrix = gate_proj[0]
    up_matrix = up_proj[0]
    down_matrix = down_proj[0]
    hidden_width = gate_matrix.shape[1]
    capacity = CAP
    slot_count = window_size * capacity
    expert_range = jnp.arange(window_size, dtype=jnp.int32)
    onehot = (expert_ids[:, :, None] == expert_range[None, None, :]).astype(jnp.bfloat16)
    per_token = jnp.sum(onehot, axis=1)
    token_range = jnp.arange(token_count, dtype=jnp.int32)
    strict_lower = (token_range[:, None] > token_range[None, :]).astype(jnp.bfloat16)
    earlier = jnp.dot(strict_lower, per_token, preferred_element_type=jnp.float32)
    slot_pick = jnp.sum(onehot.astype(jnp.float32) * earlier[:, None, :], axis=2).astype(jnp.int32)
    target = jnp.where(expert_ids < window_size, expert_ids * capacity + slot_pick, -1)
    slot_range = jnp.arange(slot_count, dtype=jnp.int32)
    pick_rows = jnp.zeros((slot_count, token_count), jnp.float32)
    combine_weights = jnp.zeros((token_count, slot_count), jnp.float32)
    for position in range(expert_ids.shape[1]):
        matches = (target[:, position][:, None] == slot_range[None, :]).astype(jnp.float32)
        pick_rows = pick_rows + matches.T
        combine_weights = combine_weights + route_gates[:, position][:, None] * matches
    pick_half = pick_rows.astype(jnp.bfloat16)
    send_rows = jnp.dot(pick_half, activations, preferred_element_type=jnp.float32).astype(
        jnp.bfloat16
    )
    send_rows = send_rows.reshape(window_size, capacity, model_width)
    slot_gate = jnp.sum(combine_weights, axis=0)
    send_cot = jnp.dot(pick_half, cotangent, preferred_element_type=jnp.float32)
    scaled = (
        (slot_gate[:, None] * send_cot)
        .astype(jnp.bfloat16)
        .reshape(window_size, capacity, model_width)
    )

    def forward_rows(input_rows):
        gate_pre = jnp.dot(input_rows, gate_matrix, preferred_element_type=jnp.float32)
        up_pre = jnp.dot(input_rows, up_matrix, preferred_element_type=jnp.float32)
        activated = (jax.nn.silu(gate_pre) * up_pre).astype(jnp.bfloat16)
        output_rows = contract_cols(activated, down_matrix).astype(jnp.bfloat16)
        return (output_rows, activated, gate_pre, up_pre)

    def backward_rows(go_rows, gate_rows, up_rows):
        back_act = jnp.dot(go_rows, down_matrix, preferred_element_type=jnp.float32)
        sigmoid_gate = jax.nn.sigmoid(gate_rows)
        grad_up_rows = (back_act * jax.nn.silu(gate_rows)).astype(jnp.bfloat16)
        grad_gate_rows = (
            back_act * up_rows * sigmoid_gate * (1.0 + gate_rows * (1.0 - sigmoid_gate))
        ).astype(jnp.bfloat16)
        grad_rows = (
            contract_cols(grad_gate_rows, gate_matrix) + contract_cols(grad_up_rows, up_matrix)
        ).astype(jnp.bfloat16)
        return (grad_rows, grad_gate_rows, grad_up_rows)

    received_rows = lax.all_to_all(send_rows, "expert", split_axis=0, concat_axis=0, tiled=True)
    source_count = received_rows.shape[0]
    item_count = received_rows.shape[1]
    flat_rows = received_rows.reshape(source_count * item_count, model_width)
    output_rows, acted_part, gate_part, up_part = run_rows(forward_rows, (flat_rows,))
    came_back = lax.all_to_all(
        output_rows.reshape(source_count, item_count, model_width),
        "expert",
        split_axis=0,
        concat_axis=0,
        tiled=True,
    )
    hidden_shape = (source_count, item_count, hidden_width)
    activated = acted_part.reshape(hidden_shape)
    gate_pre = gate_part.reshape(hidden_shape)
    up_pre = up_part.reshape(hidden_shape)
    got_rows = lax.all_to_all(scaled, "expert", split_axis=0, concat_axis=0, tiled=True)
    grad_part, grad_gate_rows, grad_up_rows = run_rows(
        backward_rows,
        (
            got_rows.reshape(slot_count, model_width),
            gate_pre.reshape(slot_count, hidden_width),
            up_pre.reshape(slot_count, hidden_width),
        ),
    )
    sent_back = lax.all_to_all(
        grad_part.reshape(window_size, capacity, model_width),
        "expert",
        split_axis=0,
        concat_axis=0,
        tiled=True,
    )
    weights_high = combine_weights.astype(jnp.bfloat16)
    weights_low = (combine_weights - weights_high.astype(jnp.float32)).astype(jnp.bfloat16)
    returned_flat = came_back.reshape(slot_count, model_width)
    layer_out = (
        jnp.dot(weights_high, returned_flat, preferred_element_type=jnp.float32)
        + jnp.dot(weights_low, returned_flat, preferred_element_type=jnp.float32)
    ).astype(jnp.bfloat16)
    grad_input = jnp.dot(
        pick_half.T, sent_back.reshape(slot_count, model_width), preferred_element_type=jnp.float32
    ).astype(jnp.bfloat16)
    go_flat = got_rows.reshape(slot_count, model_width)
    input_flat = received_rows.reshape(slot_count, model_width)
    acted_flat = activated.reshape(slot_count, hidden_width)
    hidden_grads = jnp.concatenate([grad_gate_rows, grad_up_rows], axis=1)
    summed = lax.psum_scatter(
        jnp.concatenate(
            [contract_rows(input_flat, hidden_grads), contract_rows(go_flat, acted_flat)], axis=1
        ).astype(jnp.bfloat16),
        "dp",
        scatter_dimension=0,
        tiled=True,
    ).astype(jnp.float32)
    grad_gate = summed[:, :hidden_width].astype(jnp.bfloat16)[None]
    grad_up = summed[:, hidden_width : 2 * hidden_width].astype(jnp.bfloat16)[None]
    grad_down = summed[:, 2 * hidden_width :].astype(jnp.bfloat16)[None]
    return (layer_out, grad_input, grad_gate, grad_up, grad_down)


def solution(mesh):
    in_specs = (
        P(("dp", "expert"), None),
        P(("dp", "expert"), None),
        P(("dp", "expert"), None),
        P("expert", None, None),
        P("expert", None, None),
        P("expert", None, None),
        P(("dp", "expert"), None),
    )
    out_specs = (
        P(("dp", "expert"), None),
        P(("dp", "expert"), None),
        P("expert", "dp", None),
        P("expert", "dp", None),
        P("expert", "dp", None),
    )
    return jax.shard_map(shards, mesh=mesh, in_specs=in_specs, out_specs=out_specs, check_vma=False)
```

profile of v0, /device:TPU:1, one launch (start us, length us, event | category | flops | bytes accessed | tf_op | source)
XLA Modules:
  0.0 234.4 jit_solution(13744529362736349510)
XLA Ops:
  7.2 0.0 copy-start
  7.2 1.0 slice_bitcast_fusion.17
  8.2 0.8 fusion.23
  8.9 0.1 fusion.24
  9.1 0.7 multiply_reduce_fusion
  9.8 0.7 add_select_fusion
  10.5 0.4 fusion.29
  10.9 2.8 %multiply_convert_fusion = bf16[384,2048]{1,0:T(8,128)(2,1)} fusion(bf16[128,2048]{1,0:T(8,128)(2,1)} %param.13, f32[384]{0:T(512)S(1)} %fusion.29, s32[128]{0:T(128)S(1)} %get-tuple-element.35, s32[128]{0:T(128)S(1)} %get-tuple-element.36, s32[128]{0:T(128)S(1)} %get-tuple-element.37, s32[128]{0:T(128)S(1)} %get-tuple-element.38, ...), kind=kOutput, calls=%fused_computation.16 | convolution fusion | flops 204079104 | bytes 2102784 | tf_op jit(solution)/shard_map/dot_general | solution.py:56
  13.7 3.6 %reshape.43 = bf16[32,12,2048]{2,1,0:T(8,128)(2,1)} reshape(bf16[384,2048]{1,0:T(8,128)(2,1)} %multiply_convert_fusion) | data formatting | bytes 3145728 | tf_op jit(solution)/shard_map/reshape | solution.py:60
  17.3 8.6 %all-to-all-start.2 = ((bf16[32,12,2048]{2,1,0:T(8,128)(2,1)}), bf16[32,12,2048]{2,1,0:T(8,128)(2,1)}, u32[]{:S(2)}, u32[]{:S(2)}) async-start(bf16[32,12,2048]{2,1,0:T(8,128)(2,1)} %reshape.43), calls=%async_computation.2 | async-start | bytes 4194304 | tf_op jit(solution)/shard_map/all_to_all | solution.py:98
  26.0 2.8 %convolution_convert_fusion.2 = bf16[384,2048]{1,0:T(8,128)(2,1)} fusion(bf16[128,2048]{1,0:T(8,128)(2,1)} %param.7, s32[128]{0:T(128)S(1)} %get-tuple-element.35, s32[128]{0:T(128)S(1)} %get-tuple-element.36, s32[128]{0:T(128)S(1)} %get-tuple-element.37, s32[128]{0:T(128)S(1)} %get-tuple-element.38, s32[128]{0:T(128)S(1)} %get-tuple-element.39, ...), kind=kOutput, calls=%fused_computation.18 | convolution fusion | flops 203292672 | bytes 2101248 | tf_op jit(solution)/shard_map/dot_general | solution.py:51
  28.8 3.6 %reshape.39 = bf16[32,12,2048]{2,1,0:T(8,128)(2,1)} reshape(bf16[384,2048]{1,0:T(8,128)(2,1)} %convolution_convert_fusion.2) | data formatting | bytes 3145728 | tf_op jit(solution)/shard_map/reshape | solution.py:54
  32.4 21.5 %all-to-all-done.2 = bf16[32,12,2048]{2,1,0:T(8,128)(2,1)} async-done(((bf16[32,12,2048]{2,1,0:T(8,128)(2,1)}), bf16[32,12,2048]{2,1,0:T(8,128)(2,1)}, u32[]{:S(2)}, u32[]{:S(2)}) %all-to-all-start.2) | async-done | bytes 1572896 | tf_op jit(solution)/shard_map/all_to_all | solution.py:98
  53.9 6.7 %all-to-all-start = ((bf16[32,12,2048]{2,1,0:T(8,128)(2,1)}), bf16[32,12,2048]{2,1,0:T(8,128)(2,1)}, u32[]{:S(2)}, u32[]{:S(2)}) async-start(bf16[32,12,2048]{2,1,0:T(8,128)(2,1)} %reshape.39), calls=%async_computation | async-start | bytes 4194304 | tf_op jit(solution)/shard_map/all_to_all | solution.py:82
  60.6 0.2 reduce-scatter.2.cloned.1.call-start
  60.8 3.6 %reshape.44 = bf16[384,2048]{1,0:T(8,128)(2,1)} reshape(bf16[32,12,2048]{2,1,0:T(8,128)(2,1)} %all-to-all-done.2) | data formatting | bytes 3145728 | tf_op jit(solution)/shard_map/reshape | solution.py:102
  64.5 4.8 %fusion = f32[384,768]{1,0:T(8,128)} fusion(bf16[384,2048]{1,0:T(8,128)(2,1)} %reshape.44, bf16[1,2048,768]{2,1,0:T(8,128)(2,1)} %param.12), kind=kOutput, calls=%fused_computation.3 | convolution fusion | flops 1207959552 | bytes 5898240 | tf_op jit(solution)/shard_map/dot_general | solution.py:71
  69.3 19.3 %all-to-all-done = bf16[32,12,2048]{2,1,0:T(8,128)(2,1)} async-done(((bf16[32,12,2048]{2,1,0:T(8,128)(2,1)}), bf16[32,12,2048]{2,1,0:T(8,128)(2,1)}, u32[]{:S(2)}, u32[]{:S(2)}) %all-to-all-start) | async-done | bytes 1572896 | tf_op jit(solution)/shard_map/all_to_all | solution.py:82
  88.6 3.6 %reshape.40 = bf16[384,2048]{1,0:T(8,128)(2,1)} reshape(bf16[32,12,2048]{2,1,0:T(8,128)(2,1)} %all-to-all-done) | data formatting | bytes 3145728 | tf_op jit(solution)/shard_map/reshape | solution.py:85
  92.2 3.9 %fusion.6 = f32[384,768]{1,0:T(8,128)S(1)} fusion(bf16[384,2048]{1,0:T(8,128)(2,1)} %reshape.40, bf16[1,2048,768]{2,1,0:T(8,128)(2,1)} %param.11), kind=kOutput, calls=%fused_computation.9 | convolution fusion | flops 1207959552 | bytes 5898240 | tf_op jit(solution)/shard_map/dot_general | solution.py:65
  96.1 0.0 copy-done
  96.1 0.0 copy-done.3
  96.1 0.0 copy-done.7
  96.2 0.0 copy-start.2
  96.2 1.8 multiply_convert_fusion.2
  98.0 1.9 convolution_convert_fusion.1
  99.9 3.8 %convolution_convert_fusion = bf16[2048,1536]{0,1:T(8,128)(2,1)S(1)} fusion(bf16[384,2048]{1,0:T(8,128)(2,1)S(1)} %copy-done.3, bf16[384,768]{1,0:T(8,128)(2,1)S(1)} %get-tuple-element.21, bf16[384,768]{1,0:T(8,128)(2,1)S(1)} %get-tuple-element.20), kind=kOutput, calls=%fused_computation.1 | convolution fusion | flops 2421424128 | bytes 9043968 | tf_op jit(solution)/shard_map/dot_general | solution.py:10
  103.7 11.6 %pad_maximum_fusion = bf16[2048,2304]{0,1:T(8,128)(2,1)} fusion(bf16[2048,768]{0,1:T(8,128)(2,1)S(1)} %convolution_convert_fusion.1, bf16[2048,1536]{0,1:T(8,128)(2,1)S(1)} %convolution_convert_fusion), kind=kLoop, calls=%fused_computation | loop fusion | flops 18874368 | bytes 18874368 | tf_op jit(solution)/shard_map/concatenate | solution.py:129
  115.3 0.0 reduce-scatter.2.cloned.1.call-update
  115.3 4.7 %fusion.14 = bf16[384,2048]{1,0:T(8,128)(2,1)} fusion(bf16[384,768]{1,0:T(8,128)(2,1)} %copy-done.6, bf16[1,2048,768]{2,1,0:T(8,128)(2,1)} %param.12), kind=kOutput, calls=%fused_computation.17 | convolution fusion | flops 1208745984 | bytes 5308416 | tf_op jit(solution)/shard_map/dot_general | solution.py:16
  120.0 3.6 %reshape.41 = bf16[32,12,2048]{2,1,0:T(8,128)(2,1)} reshape(bf16[384,2048]{1,0:T(8,128)(2,1)} %fusion.14) | data formatting | bytes 3145728 | tf_op jit(solution)/shard_map/reshape | solution.py:88
  123.6 6.8 %all-to-all-start.1 = ((bf16[32,12,2048]{2,1,0:T(8,128)(2,1)}), bf16[32,12,2048]{2,1,0:T(8,128)(2,1)}, u32[]{:S(2)}, u32[]{:S(2)}) async-start(bf16[32,12,2048]{2,1,0:T(8,128)(2,1)} %reshape.41), calls=%async_computation.1 | async-start | bytes 4194304 | tf_op jit(solution)/shard_map/all_to_all | solution.py:87
  130.4 3.5 %fusion.4 = f32[384,2048]{1,0:T(8,128)S(1)} fusion(bf16[384,768]{1,0:T(8,128)(2,1)} %copy-done.8, bf16[1,2048,768]{2,1,0:T(8,128)(2,1)} %param.11), kind=kOutput, calls=%fused_computation.7 | convolution fusion | flops 1207959552 | bytes 6881280 | tf_op jit(solution)/shard_map/dot_general | solution.py:16
  133.9 2.6 %add_convert_fusion = bf16[384,2048]{1,0:T(8,128)(2,1)} fusion(f32[384,2048]{1,0:T(8,128)S(1)} %fusion.4, bf16[384,768]{1,0:T(8,128)(2,1)S(1)} %copy-done.5, bf16[1,2048,768]{2,1,0:T(8,128)(2,1)S(1)} %copy-done), kind=kOutput, calls=%fused_computation.15 | convolution fusion | flops 1209532416 | bytes 8454144 | tf_op jit(solution)/shard_map/dot_general | solution.py:16
  136.5 3.6 %reshape.45 = bf16[32,12,2048]{2,1,0:T(8,128)(2,1)} reshape(bf16[384,2048]{1,0:T(8,128)(2,1)} %add_convert_fusion) | data formatting | bytes 3145728 | tf_op jit(solution)/shard_map/reshape | solution.py:108
  140.1 18.1 %all-to-all-done.1 = bf16[32,12,2048]{2,1,0:T(8,128)(2,1)} async-done(((bf16[32,12,2048]{2,1,0:T(8,128)(2,1)}), bf16[32,12,2048]{2,1,0:T(8,128)(2,1)}, u32[]{:S(2)}, u32[]{:S(2)}) %all-to-all-start.1) | async-done | bytes 1572896 | tf_op jit(solution)/shard_map/all_to_all | solution.py:87
  158.2 6.9 %all-to-all-start.3 = ((bf16[32,12,2048]{2,1,0:T(8,128)(2,1)}), bf16[32,12,2048]{2,1,0:T(8,128)(2,1)}, u32[]{:S(2)}, u32[]{:S(2)}) async-start(bf16[32,12,2048]{2,1,0:T(8,128)(2,1)} %reshape.45), calls=%async_computation.3 | async-start | bytes 4194304 | tf_op jit(solution)/shard_map/all_to_all | solution.py:107
  165.1 3.6 %reshape.42 = bf16[384,2048]{1,0:T(8,128)(2,1)} reshape(bf16[32,12,2048]{2,1,0:T(8,128)(2,1)} %all-to-all-done.1) | data formatting | bytes 3145728 | tf_op jit(solution)/shard_map/reshape | solution.py:116
  168.8 24.3 %all-to-all-done.3 = bf16[32,12,2048]{2,1,0:T(8,128)(2,1)} async-done(((bf16[32,12,2048]{2,1,0:T(8,128)(2,1)}), bf16[32,12,2048]{2,1,0:T(8,128)(2,1)}, u32[]{:S(2)}, u32[]{:S(2)}) %all-to-all-start.3) | async-done | bytes 1572896 | tf_op jit(solution)/shard_map/all_to_all | solution.py:107
  193.1 3.6 %reshape.46 = bf16[384,2048]{1,0:T(8,128)(2,1)} reshape(bf16[32,12,2048]{2,1,0:T(8,128)(2,1)} %all-to-all-done.3) | data formatting | bytes 3145728 | tf_op jit(solution)/shard_map/reshape | solution.py:122
  196.7 2.9 %convolution_convert_fusion.3 = bf16[128,2048]{1,0:T(8,128)(2,1)} fusion(bf16[384,2048]{1,0:T(8,128)(2,1)} %reshape.46, s32[128]{0:T(128)S(1)} %get-tuple-element.35, s32[128]{0:T(128)S(1)} %get-tuple-element.36, s32[128]{0:T(128)S(1)} %get-tuple-element.37, s32[128]{0:T(128)S(1)} %get-tuple-element.38, s32[128]{0:T(128)S(1)} %get-tuple-element.39, ...), kind=kOutput, calls=%fused_computation.21 | convolution fusion | flops 202768384 | bytes 2101248 | tf_op jit(solution)/shard_map/dot_general | solution.py:121
  199.6 0.7 fusion.26
  200.4 1.5 fusion.17
  201.9 18.7 %reduce-scatter.2.cloned.1.call-done = bf16[256,2304]{0,1:T(8,128)(2,1)} async-done(((bf16[2048,2304]{0,1:T(8,128)(2,1)}), bf16[256,2304]{0,1:T(8,128)(2,1)}) %reduce-scatter.2.cloned.1.call-update) | async-done | bytes 1179664 | tf_op jit(solution)/shard_map/reduce_scatter | solution.py:128
  220.6 2.2 slice_bitcast_fusion
  222.8 1.9 copy.24
  224.7 1.9 copy.23
  226.7 0.9 copy.22
  (14 shorter events, 0.0 us)
Async XLA Ops:
  7.2 89.0 %copy-start = (bf16[1,2048,768]{2,1,0:T(8,128)(2,1)S(1)}, bf16[1,2048,768]{2,1,0:T(8,128)(2,1)}, u32[]{:S(2)}) copy-start(bf16[1,2048,768]{2,1,0:T(8,128)(2,1)} %param.10) | copy-start | bytes 9437188
  17.3 36.5 %all-to-all-start.2 = ((bf16[32,12,2048]{2,1,0:T(8,128)(2,1)}), bf16[32,12,2048]{2,1,0:T(8,128)(2,1)}, u32[]{:S(2)}, u32[]{:S(2)}) async-start(bf16[32,12,2048]{2,1,0:T(8,128)(2,1)} %reshape.43), calls=%async_computation.2 | async-start | bytes 4194304 | tf_op jit(solution)/shard_map/all_to_all | solution.py:98
  53.9 34.7 %all-to-all-start = ((bf16[32,12,2048]{2,1,0:T(8,128)(2,1)}), bf16[32,12,2048]{2,1,0:T(8,128)(2,1)}, u32[]{:S(2)}, u32[]{:S(2)}) async-start(bf16[32,12,2048]{2,1,0:T(8,128)(2,1)} %reshape.39), calls=%async_computation | async-start | bytes 4194304 | tf_op jit(solution)/shard_map/all_to_all | solution.py:82
  60.6 160.0 %reduce-scatter.2.cloned.1.call-start = ((), (), s32[]{:S(2)}) async-start(), calls=%async_computation.5 | async-start | bytes 10616832 | tf_op jit(solution)/shard_map/reduce_scatter | solution.py:128
  92.2 3.9 %copy-start.3 = (bf16[384,2048]{1,0:T(8,128)(2,1)S(1)}, bf16[384,2048]{1,0:T(8,128)(2,1)}, u32[]{:S(2)}) copy-start(bf16[384,2048]{1,0:T(8,128)(2,1)} %reshape.40) | copy-start | bytes 4718596
  92.2 3.9 %copy-start.7 = (f32[384,768]{1,0:T(8,128)S(1)}, f32[384,768]{1,0:T(8,128)}, u32[]{:S(2)}) copy-start(f32[384,768]{1,0:T(8,128)} %fusion) | copy-start | bytes 3538948
  96.2 1.9 copy-start.2
  98.0 1.9 copy-start.6
  98.0 1.9 copy-start.4
  98.0 1.9 copy-start.8
  123.6 34.6 %all-to-all-start.1 = ((bf16[32,12,2048]{2,1,0:T(8,128)(2,1)}), bf16[32,12,2048]{2,1,0:T(8,128)(2,1)}, u32[]{:S(2)}, u32[]{:S(2)}) async-start(bf16[32,12,2048]{2,1,0:T(8,128)(2,1)} %reshape.41), calls=%async_computation.1 | async-start | bytes 4194304 | tf_op jit(solution)/shard_map/all_to_all | solution.py:87
  130.4 3.6 %copy-start.5 = (bf16[384,768]{1,0:T(8,128)(2,1)S(1)}, bf16[384,768]{1,0:T(8,128)(2,1)}, u32[]{:S(2)}) copy-start(bf16[384,768]{1,0:T(8,128)(2,1)} %copy-done.4) | copy-start | bytes 1769476
  158.2 34.9 %all-to-all-start.3 = ((bf16[32,12,2048]{2,1,0:T(8,128)(2,1)}), bf16[32,12,2048]{2,1,0:T(8,128)(2,1)}, u32[]{:S(2)}, u32[]{:S(2)}) async-start(bf16[32,12,2048]{2,1,0:T(8,128)(2,1)} %reshape.45), calls=%async_computation.3 | async-start | bytes 4194304 | tf_op jit(solution)/shard_map/all_to_all | solution.py:107
  196.7 2.9 %copy-start.1 = (bf16[384,2048]{1,0:T(8,128)(2,1)S(1)}, bf16[384,2048]{1,0:T(8,128)(2,1)}, u32[]{:S(2)}) copy-start(bf16[384,2048]{1,0:T(8,128)(2,1)} %reshape.42) | copy-start | bytes 4718596
Sparse Core Ops, SparseCore 0:
  115.4 105.1 reduce-scatter.1
where the time goes:
time: 236 us; the launch traced here: 234 us
  waiting for transfers between devices  102 us (43%)
  matrix products  37.9 us (16%)
  local copies, waits for them, and re-layouts  37 us (16%)
  starting transfers between devices  29.2 us (12%)
  between operations  14.2 us (6%)
  other arithmetic  14.1 us (6%)
    all_to_all x1, waiting for transfers between devices, shards(): lax.all_to_all(grad_part.reshape(window_size, capacity, model_width), 'ex...  24.3 us
    all_to_all x1, waiting for transfers between devices, shards(): lax.all_to_all(scaled, 'expert', split_axis=0, concat_axis=0, tiled=True)  21.5 us
    all_to_all x1, waiting for transfers between devices, shards(): lax.all_to_all(send_rows, 'expert', split_axis=0, concat_axis=0, tiled=True)  19.3 us
    reduce_scatter x1, waiting for transfers between devices, shards(): lax.psum_scatter(jnp.concatenate([contract_rows(input_flat, hidden_grads)...  18.7 us
    all_to_all x1, waiting for transfers between devices, shards(): lax.all_to_all(output_rows.reshape(source_count, item_count, model_width)...  18.1 us
    concatenate x1, other arithmetic, shards(): jnp.concatenate([contract_rows(input_flat, hidden_grads), contract_rows(g...  11.6 us
    dot_general x3, matrix products, contract_cols(): lax.dot_general(left_side, right_side, (((1,), (1,)), ((), ())), preferre...  10.8 us
    all_to_all x1, starting transfers between devices, shards(): lax.all_to_all(scaled, 'expert', split_axis=0, concat_axis=0, tiled=True)  8.64 us
  transfers between devices with their start and end apart: 5, of which 5 were waited for; matrix products, arithmetic and copies ran while one was open for 19% of the time, Pallas kernels for 0%

commit v1 on v0

v1 whole, which is shorter than its diff:
```python
import functools

import jax
import jax.numpy as jnp
import numpy as np
from jax import lax
from jax.experimental import pallas as pl
from jax.experimental.pallas import tpu as pltpu
from jax.sharding import PartitionSpec as P

MESH = pl.DeviceIdType.MESH
BF16 = jnp.bfloat16
F32 = jnp.float32

CAP = 12
NE = 32
ND = 8
TOK = 128
TOP = 8
D = 2048
FF = 768
SLOTS = NE * CAP
GROUP = 8
NG = NE // GROUP
NQ = 4
QW = D // NQ
GR = GROUP * CAP
PR = CAP * NQ
DC = D // ND
HALF = FF // 2
TILE = 256


def dot(a, b):
    return jnp.dot(a, b, preferred_element_type=F32)


def dot_t(a, b):
    return lax.dot_general(a, b, (((1,), (1,)), ((), ())), preferred_element_type=F32)


def constants():
    j = np.arange(SLOTS)
    expand = (j[:, None] // CAP == np.arange(NE)[None, :]).astype(np.float32)
    slot_row = np.broadcast_to((j % CAP)[:, None], (SLOTS, TOK)).astype(np.float32)
    rows = np.arange(GROUP * PR)
    q, rest = rows // GR, rows % GR
    source = (rest // CAP) * PR + q * CAP + rest % CAP
    unshuffle = (source[:, None] == rows[None, :]).astype(np.float32)
    return (
        jnp.asarray(expand, BF16),
        jnp.asarray(slot_row, F32),
        jnp.asarray(unshuffle, BF16),
        jnp.asarray(unshuffle.T, BF16),
    )


def kernel(
    ids_ref, gates_ref, act_ref, cot_ref, wg_hbm, wu_hbm, wd_hbm, expand_ref, row_ref, un_ref, sh_ref,
    lo_ref, gi_ref, gg_ref, gu_ref, gd_ref,
    wg, wu, wd, pick, sgate, comb, send, recv, stack, x_rows, c_rows, lt, fac, hid, rs_send, rs_recv,
    wsem, lsem, ssem, rsem, zs, zr,
):
    me = lax.axis_index("expert")
    z = lax.axis_index("dp")
    my_y, my_x, my_c = me // 8, (me // 2) % 4, me % 2

    def peer(o):
        return (((my_y + o // 8) % 4) * 4 + (my_x + (o // 2) % 4) % 4) * 2 + (my_c + o % 2) % 2

    loads = [
        pltpu.make_async_copy(src.at[0], dst, wsem.at[i])
        for i, (src, dst) in enumerate(((wg_hbm, wg), (wu_hbm, wu), (wd_hbm, wd)))
    ]
    for load in loads:
        load.start()

    barrier = pltpu.get_barrier_semaphore()

    def greet(o, _):
        pl.semaphore_signal(barrier, inc=1, device_id={"expert": peer(o)}, device_id_type=MESH)
        return 0

    lax.fori_loop(1, NE, greet, 0)
    for step in (1, ND - 1):
        pl.semaphore_signal(barrier, inc=1, device_id={"dp": (z + step) % ND}, device_id_type=MESH)

    def over_peers(f):
        def body(i, _):
            f((i + 20) % NE)
            return 0

        lax.fori_loop(0, 12, body, 0)
        lax.fori_loop(13, NE, body, 0)

    def a2a(p, o):
        to = peer(o)
        return pltpu.make_async_remote_copy(
            src_ref=send.at[p, to],
            dst_ref=recv.at[p, me],
            send_sem=ssem.at[p, o],
            recv_sem=rsem.at[p, o],
            device_id={"expert": to},
            device_id_type=MESH,
        )

    def own(p):
        return pltpu.make_async_copy(send.at[p, me], recv.at[p, me], lsem.at[p])

    def ring(m, d, s):
        return pltpu.make_async_remote_copy(
            src_ref=rs_send.at[m, d, s],
            dst_ref=rs_recv.at[m, d, s],
            send_sem=zs.at[m, d, s],
            recv_sem=zr.at[m, d, s],
            device_id={"dp": (z + 1 - 2 * d + ND) % ND},
            device_id_type=MESH,
        )

    ids = ids_ref[...]
    gates = gates_ref[...]
    experts = lax.broadcasted_iota(jnp.int32, (TOK, NE), 1)
    named = jnp.zeros((TOK, NE), F32)
    gate_of = jnp.zeros((TOK, NE), F32)
    for k in range(TOP):
        hit = ids[:, k : k + 1] == experts
        named = named + jnp.where(hit, 1.0, 0.0)
        gate_of = gate_of + jnp.where(hit, gates[:, k : k + 1], 0.0)
    earlier_than = lax.broadcasted_iota(jnp.int32, (TOK, TOK), 0) > lax.broadcasted_iota(jnp.int32, (TOK, TOK), 1)
    earlier = dot(jnp.where(earlier_than, 1.0, 0.0).astype(BF16), named.astype(BF16))
    slot_of = jnp.where(named > 0.0, earlier, -1.0).astype(BF16)
    expand = expand_ref[...]
    match = dot_t(expand, slot_of) == row_ref[...]
    high = gate_of.astype(BF16)
    rest = gate_of - high.astype(F32)
    mid = rest.astype(BF16)
    low = (rest - mid.astype(F32)).astype(BF16)
    spread = dot_t(expand, high) + dot_t(expand, mid) + dot_t(expand, low)
    weight = jnp.where(match, spread, 0.0)
    ones = jnp.where(match, 1.0, 0.0)
    pick[...] = ones.astype(BF16)
    sgate[...] = jnp.sum(weight, axis=1, keepdims=True)
    weight_t = weight.T
    weight_high = weight_t.astype(BF16)
    comb[0] = weight_high
    comb[1] = (weight_t - weight_high.astype(F32)).astype(BF16)
    comb[2] = ones.T.astype(BF16)

    def shuffle_out(p, g, stacked):
        packed = dot(sh_ref[...], stacked).astype(BF16)
        send[p, g * GROUP : (g + 1) * GROUP] = packed.reshape(GROUP, PR, QW)

    def pack(p, g, source, scaled):
        rows = dot(pick[g * GR : (g + 1) * GR, :], source[...])
        if scaled:
            rows = rows * sgate[g * GR : (g + 1) * GR, :]
        rows = rows.astype(BF16)
        shuffle_out(p, g, jnp.concatenate([rows[:, q * QW : (q + 1) * QW] for q in range(NQ)], axis=0))

    def unshuffle(p, out):
        for g in range(NG):
            block = recv[p, g * GROUP : (g + 1) * GROUP].reshape(GROUP * PR, QW)
            block = dot(un_ref[...], block).astype(BF16)
            for q in range(NQ):
                out[g * GR : (g + 1) * GR, q * QW : (q + 1) * QW] = block[q * GR : (q + 1) * GR]

    for g in range(NG):
        pack(0, g, act_ref, False)
    pl.semaphore_wait(barrier, NE - 1 + 2)
    over_peers(lambda o: a2a(0, o).start())
    own(0).start()
    for g in range(NG):
        pack(1, g, cot_ref, True)

    def next_cot(o):
        a2a(0, o).wait_send()
        a2a(1, o).start()

    over_peers(next_cot)
    own(1).start()

    over_peers(lambda o: a2a(0, o).wait_recv())
    own(0).wait()
    unshuffle(0, x_rows)
    for load in loads:
        load.wait()

    def put_hidden(m, n, value):
        for at in range(n * TILE, (n + 1) * TILE, 128):
            d, col = at // HALF, at % HALF
            hid[m, d, :, col : col + 128] = value[:, at - n * TILE : at - n * TILE + 128]

    for n in range(FF // TILE):
        cols = slice(n * TILE, (n + 1) * TILE)
        gate_pre = dot(x_rows[...], wg[:, cols])
        up_pre = dot(x_rows[...], wu[:, cols])
        sig = 1.0 / (1.0 + jnp.exp(-gate_pre))
        silu = gate_pre * sig
        fac[0, :, cols] = silu
        fac[1, :, cols] = up_pre * sig * (1.0 + gate_pre * (1.0 - sig))
        put_hidden(0, n, (silu * up_pre).astype(BF16))

    for j in range(ND):
        lt[1, j] = x_rows[:, j * DC : (j + 1) * DC].T

    def whole(m):
        return jnp.concatenate([hid[m, 0], hid[m, 1]], axis=1)

    def send_back(p, q, rows):
        for g in range(NG):
            stack[g, q * GR : (q + 1) * GR] = rows[g * GR : (g + 1) * GR].astype(BF16)

    for q in range(NQ):
        send_back(2, q, dot_t(whole(0), wd[q * QW : (q + 1) * QW, :]))
    for g in range(NG):
        shuffle_out(2, g, stack[g])

    over_peers(lambda o: a2a(1, o).wait_recv())
    own(1).wait()
    unshuffle(1, c_rows)
    for j in range(ND):
        lt[0, j] = c_rows[:, j * DC : (j + 1) * DC].T

    def chunk(d, s):
        return (z - (1 - 2 * d) * (1 + s) + 2 * ND) % ND

    def part(m, d, c):
        return dot(lt[(m + 1) // 2, c], hid[m, d])

    def first(m):
        for d in range(2):
            rs_send[m, d, 0] = part(m, d, chunk(d, 0)).astype(BF16)
            ring(m, d, 0).start()

    def steps(lowest, end):
        def body(i, _):
            s, m, d = i // 6, (i // 2) % 3, i % 2
            mine = part(m, d, chunk(d, s))
            ring(m, d, s - 1).wait_recv()
            rs_send[m, d, s] = (mine + rs_recv[m, d, s - 1].astype(F32)).astype(BF16)
            ring(m, d, s).start()
            return 0

        lax.fori_loop(6 * lowest, 6 * end, body, 0)

    first(0)
    over_peers(lambda o: a2a(2, o).start())
    own(2).start()

    for n in range(FF // TILE):
        cols = slice(n * TILE, (n + 1) * TILE)
        back = dot(c_rows[...], wd[:, cols])
        put_hidden(2, n, (back * fac[0, :, cols]).astype(BF16))
        put_hidden(1, n, (back * fac[1, :, cols]).astype(BF16))
    first(1)
    first(2)
    steps(1, 2)

    for q in range(NQ):
        rows = slice(q * QW, (q + 1) * QW)
        send_back(3, q, dot_t(whole(1), wg[rows, :]) + dot_t(whole(2), wu[rows, :]))
    for g in range(NG):
        shuffle_out(3, g, stack[g])
    over_peers(lambda o: a2a(3, o).start())
    own(3).start()

    steps(2, 4)
    over_peers(lambda o: a2a(2, o).wait_recv())
    own(2).wait()
    unshuffle(2, x_rows)
    for q in range(NQ):
        cols = slice(q * QW, (q + 1) * QW)
        lo_ref[:, cols] = (dot(comb[0], x_rows[:, cols]) + dot(comb[1], x_rows[:, cols])).astype(BF16)

    steps(4, 6)
    over_peers(lambda o: a2a(3, o).wait_recv())
    own(3).wait()
    unshuffle(3, x_rows)
    for q in range(NQ):
        cols = slice(q * QW, (q + 1) * QW)
        gi_ref[:, cols] = dot(comb[2], x_rows[:, cols]).astype(BF16)

    steps(6, 7)
    for m, out in ((0, gd_ref), (1, gg_ref), (2, gu_ref)):
        for d in range(2):
            mine = part(m, d, z)
            ring(m, d, ND - 2).wait_recv()
            out[:, d * HALF : (d + 1) * HALF] = (mine + rs_recv[m, d, ND - 2].astype(F32)).astype(BF16)

    for p in (1, 2, 3):
        over_peers(lambda o: a2a(p, o).wait_send())

    def drain(i, _):
        ring((i // 2) % 3, i % 2, i // 6).wait_send()
        return 0

    lax.fori_loop(0, 6 * (ND - 1), drain, 0)


def shards(activations, expert_ids, route_gates, gate_proj, up_proj, down_proj, cotangent):
    vmem = pl.BlockSpec(memory_space=pltpu.VMEM)
    anywhere = pl.BlockSpec(memory_space=pl.ANY)
    dma = pltpu.SemaphoreType.DMA
    out = pl.pallas_call(
        kernel,
        out_shape=(
            jax.ShapeDtypeStruct((TOK, D), BF16),
            jax.ShapeDtypeStruct((TOK, D), BF16),
            jax.ShapeDtypeStruct((DC, FF), BF16),
            jax.ShapeDtypeStruct((DC, FF), BF16),
            jax.ShapeDtypeStruct((DC, FF), BF16),
        ),
        in_specs=[vmem] * 4 + [anywhere] * 3 + [vmem] * 4,
        out_specs=(vmem,) * 5,
        scratch_shapes=[
            pltpu.VMEM((D, FF), BF16),
            pltpu.VMEM((D, FF), BF16),
            pltpu.VMEM((D, FF), BF16),
            pltpu.VMEM((SLOTS, TOK), BF16),
            pltpu.VMEM((SLOTS, 1), F32),
            pltpu.VMEM((3, TOK, SLOTS), BF16),
            pltpu.VMEM((4, NE, PR, QW), BF16),
            pltpu.VMEM((4, NE, PR, QW), BF16),
            pltpu.VMEM((NG, GROUP * PR, QW), BF16),
            pltpu.VMEM((SLOTS, D), BF16),
            pltpu.VMEM((SLOTS, D), BF16),
            pltpu.VMEM((2, ND, DC, SLOTS), BF16),
            pltpu.VMEM((2, SLOTS, FF), F32),
            pltpu.VMEM((3, 2, SLOTS, HALF), BF16),
            pltpu.VMEM((3, 2, ND - 1, DC, HALF), BF16),
            pltpu.VMEM((3, 2, ND - 1, DC, HALF), BF16),
            dma((3,)),
            dma((4,)),
            dma((4, NE)),
            dma((4, NE)),
            dma((3, 2, ND - 1)),
            dma((3, 2, ND - 1)),
        ],
        compiler_params=pltpu.CompilerParams(
            collective_id=0, has_side_effects=True, vmem_limit_bytes=60 * 2**20
        ),
        cost_estimate=pl.CostEstimate(flops=12 * 10**9, bytes_accessed=15 * 10**6, transcendentals=300000),
        name="expert_layer",
    )(expert_ids, route_gates, activations, cotangent, gate_proj, up_proj, down_proj, *constants())
    layer_out, grad_input, grad_gate, grad_up, grad_down = out
    return (layer_out, grad_input, grad_gate[None], grad_up[None], grad_down[None])


def solution(mesh):
    in_specs = (
        P(("dp", "expert"), None),
        P(("dp", "expert"), None),
        P(("dp", "expert"), None),
        P("expert", None, None),
        P("expert", None, None),
        P("expert", None, None),
        P(("dp", "expert"), None),
    )
    out_specs = (
        P(("dp", "expert"), None),
        P(("dp", "expert"), None),
        P("expert", "dp", None),
        P("expert", "dp", None),
        P("expert", "dp", None),
    )
    return jax.shard_map(shards, mesh=mesh, in_specs=in_specs, out_specs=out_specs, check_vma=False)
```

time: 236 us -> 164 us (0.69)
  Pallas kernels: 0 us -> 154 us
  waiting for transfers between devices: 102 us -> 0 us
  matrix products: 37.9 us -> 0 us
  starting transfers between devices: 29.2 us -> 0 us
  local copies, waits for them, and re-layouts: 37 us -> 9.93 us
  other arithmetic: 14.1 us -> 0 us
  between operations: 14.2 us -> 0.66 us
    pallas_call x0 -> x1, Pallas kernels: none -> 154 us  [shards(): pl.pallas_call(kernel, out_shape=(jax.ShapeDtypeStruct((TOK, D), BF16), j...]
    all_to_all x4 -> x0, waiting for transfers between devices: 83.2 us -> none  [the longest x1 24.3 us: shards(): lax.all_to_all(grad_part.reshape(window_size, capacity, model_width), 'ex...]
    dot_general x14 -> x0, matrix products: 37.9 us -> none  [the longest x3 10.8 us: contract_cols(): lax.dot_general(left_side, right_side, (((1,), (1,)), ((), ())), preferre...]
    all_to_all x4 -> x0, starting transfers between devices: 29 us -> none  [the longest x1 8.64 us: shards(): lax.all_to_all(scaled, 'expert', split_axis=0, concat_axis=0, tiled=True)]
    reshape x8 -> x0, local copies, waits for them, and re-layouts: 29 us -> none  [the longest x1 3.65 us: shards(): returned_flat = came_back.reshape(slot_count, model_width)]
    reduce_scatter x1 -> x0, waiting for transfers between devices: 18.7 us -> none  [shards(): lax.psum_scatter(jnp.concatenate([contract_rows(input_flat, hidden_grads)...]
    concatenate x1 -> x0, other arithmetic: 11.6 us -> none  [shards(): jnp.concatenate([contract_rows(input_flat, hidden_grads), contract_rows(g...]
    unnamed x21 -> x11, local copies, waits for them, and re-layouts: 4.79 us -> 9.93 us
  transfers between devices with their start and end apart: 5 -> 0, of which waited for: 5 -> 0; matrix products, arithmetic and copies ran while one was open for 19% -> 0% of each run, Pallas kernels for 0% -> 0%
where the time goes in v1:
time: 164 us
  Pallas kernels  154 us (94%)
  local copies, waits for them, and re-layouts  9.93 us (6%)
    pallas_call x1, Pallas kernels, shards(): pl.pallas_call(kernel, out_shape=(jax.ShapeDtypeStruct((TOK, D), BF16), j...  154 us
    unnamed x11, local copies, waits for them, and re-layouts  9.93 us

profile of v1, /device:TPU:1, one launch (start us, length us, event | category | flops | bytes accessed | tf_op | source)
XLA Modules:
  0.0 164.2 jit_solution(7281865030111264592)
XLA Ops:
  0.6 1.4 copy.16.ids_ref
  2.0 1.4 copy.17.gates_ref
  3.5 153.6 %expert_layer.1 = (bf16[128,2048]{1,0:T(8,128)(2,1)}, bf16[128,2048]{1,0:T(8,128)(2,1)}, bf16[256,768]{1,0:T(8,128)(2,1)}, bf16[256,768]{1,0:T(8,128)(2,1)}, bf16[256,768]{1,0:T(8,128)(2,1)}) custom-call(s32[128,8]{1,0:T(8,128)} %copy.16.ids_ref, f32[128,8]{1,0:T(8,128)} %copy.17.gates_ref, bf16[128,2048]{1,0:T(8,128)(2,1)} %act_ref.1, ...), custom_call_target="tpu_custom_call" | custom-call | flops 12000000000 | bytes 15000000 | tf_op jit(solution)/shard_map/expert_layer/pallas_call | solution.py:304
  157.1 0.0 copy-start.1
  157.1 0.0 copy-start
  157.1 2.0 %copy.23 = bf16[128,2048]{1,0:T(8,128)(2,1)} copy(bf16[128,2048]{1,0:T(8,128)(2,1)} %get-tuple-element.20) | data formatting | bytes 1048576
  159.0 1.9 %copy.24 = bf16[128,2048]{1,0:T(8,128)(2,1)} copy(bf16[128,2048]{1,0:T(8,128)(2,1)} %get-tuple-element.21) | data formatting | bytes 1048576
  160.9 1.8 %copy.25 = bf16[1,256,768]{2,1,0:T(8,128)(2,1)} copy(bf16[1,256,768]{2,1,0:T(8,128)(2,1)} %bitcast.5) | data formatting | bytes 786432
  162.7 0.0 copy-done.1
  162.7 0.7 copy.26
  163.4 0.0 copy-done
  163.4 0.7 copy.27
Async XLA Ops:
  157.1 5.6 %copy-start.1 = (bf16[256,768]{1,0:T(8,128)(2,1)S(1)}, bf16[256,768]{1,0:T(8,128)(2,1)}, u32[]{:S(2)}) copy-start(bf16[256,768]{1,0:T(8,128)(2,1)} %get-tuple-element.13) | copy-start | bytes 1179652
  157.1 6.4 %copy-start = (bf16[256,768]{1,0:T(8,128)(2,1)S(1)}, bf16[256,768]{1,0:T(8,128)(2,1)}, u32[]{:S(2)}) copy-start(bf16[256,768]{1,0:T(8,128)(2,1)} %get-tuple-element.14) | copy-start | bytes 1179652

commit v2 on v1

v2 whole, which is shorter than its diff:
```python
import functools

import jax
import jax.numpy as jnp
import numpy as np
from jax import lax
from jax.experimental import pallas as pl
from jax.experimental.pallas import tpu as pltpu
from jax.sharding import PartitionSpec as P

MESH = pl.DeviceIdType.MESH
BF16 = jnp.bfloat16
F32 = jnp.float32

CAP = 12
NE = 32
ND = 8
TOK = 128
TOP = 8
D = 2048
FF = 768
SLOTS = NE * CAP
GROUP = 8
NG = NE // GROUP
NQ = 4
QW = D // NQ
GR = GROUP * CAP
PIECE = 16
NP = CAP * NQ // PIECE
DC = D // ND
HALF = FF // 2
TILE = 256


def dot(a, b):
    return jnp.dot(a, b, preferred_element_type=F32)


def dot_t(a, b):
    return lax.dot_general(a, b, (((1,), (1,)), ((), ())), preferred_element_type=F32)


def constants():
    table = np.zeros((NP, GROUP * PIECE, 2 * GR), np.float32)
    for p in range(NP):
        for s in range(GROUP):
            for u in range(PIECE):
                q, r = divmod(p * PIECE + u, CAP)
                table[p, s * PIECE + u, (q - p) * GR + s * CAP + r] = 1.0
    return jnp.asarray(table, BF16), jnp.asarray(table.transpose(0, 2, 1), BF16)


def kernel(
    ids_ref, gates_ref, act_hbm, cot_hbm, wg_hbm, wu_hbm, wd_hbm, to_hbm, from_hbm,
    lo_hbm, gi_hbm, gg_hbm, gu_hbm, gd_hbm,
    act, cot, wg, wu, wd, to_piece, from_piece, pick, sgate, comb, send, recv, stack, x_rows, c_rows,
    lt, fac, hid, rs_send, rs_recv, tokens_out, grads_out,
    wsem, osem, lsem, ssem, rsem, csem, crem, zs, zr,
):
    me = lax.axis_index("expert")
    z = lax.axis_index("dp")
    my_y, my_x, my_c = me // 8, (me // 2) % 4, me % 2

    def peer(o):
        return (((my_y + o // 8) % 4) * 4 + (my_x + (o // 2) % 4) % 4) * 2 + (my_c + o % 2) % 2

    barrier = pltpu.get_barrier_semaphore()

    def greet(o, _):
        pl.semaphore_signal(barrier, inc=1, device_id={"expert": peer(o)}, device_id_type=MESH)
        return 0

    lax.fori_loop(1, NE, greet, 0)
    for step in (1, ND - 1):
        pl.semaphore_signal(barrier, inc=1, device_id={"dp": (z + step) % ND}, device_id_type=MESH)

    sources = (
        (act_hbm, act), (to_hbm, to_piece), (cot_hbm, cot), (from_hbm, from_piece),
        (wg_hbm.at[0], wg), (wu_hbm.at[0], wu), (wd_hbm.at[0], wd),
    )
    loads = [pltpu.make_async_copy(a, b, wsem.at[i]) for i, (a, b) in enumerate(sources)]
    for load in loads:
        load.start()

    def over_peers(f):
        def body(i, _):
            f((i + 20) % NE)
            return 0

        lax.fori_loop(0, 12, body, 0)
        lax.fori_loop(13, NE, body, 0)

    def a2a(p, o):
        to = peer(o)
        return pltpu.make_async_remote_copy(
            src_ref=send.at[p, to],
            dst_ref=recv.at[p, me],
            send_sem=ssem.at[p, o],
            recv_sem=rsem.at[p, o],
            device_id={"expert": to},
            device_id_type=MESH,
        )

    def a2a_piece(t, o):
        to = peer(o)
        return pltpu.make_async_remote_copy(
            src_ref=send.at[1, to, t],
            dst_ref=recv.at[1, me, t],
            send_sem=csem.at[t, o],
            recv_sem=crem.at[t, o],
            device_id={"expert": to},
            device_id_type=MESH,
        )

    def own(p):
        return pltpu.make_async_copy(send.at[p, me], recv.at[p, me], lsem.at[p])

    def ring(m, d, s):
        return pltpu.make_async_remote_copy(
            src_ref=rs_send.at[m, d, s],
            dst_ref=rs_recv.at[m, d, s],
            send_sem=zs.at[m, d, s],
            recv_sem=zr.at[m, d, s],
            device_id={"dp": (z + 1 - 2 * d + ND) % ND},
            device_id_type=MESH,
        )

    def chunk(d, s):
        return (z - (1 - 2 * d) * (1 + s) + 2 * ND) % ND

    chunks = [(chunk(0, i), chunk(1, i) if i < NQ - 1 else z) for i in range(NQ)]

    ids = ids_ref[...]
    gates = gates_ref[...]
    experts = lax.broadcasted_iota(jnp.int32, (NE, TOK), 0)
    named = jnp.zeros((NE, TOK), F32)
    gate_of = jnp.zeros((NE, TOK), F32)
    for k in range(TOP):
        hit = ids[k : k + 1, :] == experts
        named = named + jnp.where(hit, 1.0, 0.0)
        gate_of = gate_of + jnp.where(hit, gates[k : k + 1, :], 0.0)
    before = lax.broadcasted_iota(jnp.int32, (TOK, TOK), 0) < lax.broadcasted_iota(jnp.int32, (TOK, TOK), 1)
    earlier = dot(named.astype(BF16), jnp.where(before, 1.0, 0.0).astype(BF16))
    slot_of = jnp.where(named > 0.0, earlier, -1.0).astype(BF16)
    slots = lax.broadcasted_iota(jnp.int32, (SLOTS, NE), 0)
    first_slot = lax.broadcasted_iota(jnp.int32, (SLOTS, NE), 1) * CAP
    expand = jnp.where((slots >= first_slot) & (slots < first_slot + CAP), 1.0, 0.0)
    row = jnp.sum(expand * (slots - first_slot).astype(F32), axis=1, keepdims=True)
    expand = expand.astype(BF16)
    match = dot(expand, slot_of) == row
    high = gate_of.astype(BF16)
    rest = gate_of - high.astype(F32)
    mid = rest.astype(BF16)
    low = (rest - mid.astype(F32)).astype(BF16)
    ones = jnp.where(match, 1.0, 0.0)
    pick[...] = ones.astype(BF16)

    def shuffle_out(p, g, block):
        for t in range(NP):
            both = jnp.concatenate([block(t), block(t + 1)], axis=0)
            packed = dot(to_piece[t], both).astype(BF16)
            send[p, g * GROUP : (g + 1) * GROUP, t] = packed.reshape(GROUP, PIECE, QW)

    def unshuffle(p, q):
        out = []
        for g in range(NG):
            def piece(t):
                return recv[p, g * GROUP : (g + 1) * GROUP, t].reshape(GROUP * PIECE, QW)

            total = None
            if q < NP:
                total = dot(from_piece[q, :GR, :], piece(q))
            if q > 0:
                more = dot(from_piece[q - 1, GR:, :], piece(q - 1))
                total = more if total is None else total + more
            out.append(total.astype(BF16))
        return out

    def unshuffle_all(p):
        for q in range(NQ):
            for g, rows in enumerate(unshuffle(p, q)):
                x_rows[g * GR : (g + 1) * GR, q * QW : (q + 1) * QW] = rows

    loads[0].wait()
    loads[1].wait()
    for g in range(NG):
        rows = dot(pick[g * GR : (g + 1) * GR, :], act[...]).astype(BF16)
        shuffle_out(0, g, lambda q: rows[:, q * QW : (q + 1) * QW])
    pl.semaphore_wait(barrier, NE - 1 + 2)
    over_peers(lambda o: a2a(0, o).start())
    own(0).start()

    spread = dot(expand, high) + dot(expand, mid) + dot(expand, low)
    weight = jnp.where(match, spread, 0.0)
    sgate[...] = jnp.sum(weight, axis=1, keepdims=True)
    weight_t = weight.T
    weight_high = weight_t.astype(BF16)
    comb[0] = weight_high
    comb[1] = (weight_t - weight_high.astype(F32)).astype(BF16)
    comb[2] = ones.T.astype(BF16)

    loads[2].wait()
    for g in range(NG):
        def scaled(i):
            cols = [
                dot(pick[g * GR : (g + 1) * GR, :], cot[:, pl.ds(pl.multiple_of(c * DC, DC), DC)])
                for c in chunks[i]
            ]
            return (jnp.concatenate(cols, axis=1) * sgate[g * GR : (g + 1) * GR, :]).astype(BF16)

        blocks = [scaled(i) for i in range(NQ)]
        shuffle_out(1, g, lambda q: blocks[q])
    own(1).start()

    def next_cot(o):
        a2a(0, o).wait_send()
        a2a_piece(0, o).start()

    over_peers(next_cot)

    for load in loads[3:]:
        load.wait()
    over_peers(lambda o: a2a(0, o).wait_recv())
    own(0).wait()
    unshuffle_all(0)

    def put_hidden(m, n, value):
        for at in range(n * TILE, (n + 1) * TILE, 128):
            d, col = at // HALF, at % HALF
            hid[m, d, :, col : col + 128] = value[:, at - n * TILE : at - n * TILE + 128]

    for n in range(FF // TILE):
        cols = slice(n * TILE, (n + 1) * TILE)
        gate_pre = dot(x_rows[...], wg[:, cols])
        up_pre = dot(x_rows[...], wu[:, cols])
        sig = 1.0 / (1.0 + jnp.exp(-gate_pre))
        silu = gate_pre * sig
        fac[0, :, cols] = silu
        fac[1, :, cols] = up_pre * sig * (1.0 + gate_pre * (1.0 - sig))
        put_hidden(0, n, (silu * up_pre).astype(BF16))

    over_peers(lambda o: a2a_piece(1, o).start())

    def take_cot(i):
        for g, rows in enumerate(unshuffle(1, i)):
            for h, c in enumerate(chunks[i]):
                at = pl.ds(pl.multiple_of(c * DC, DC), DC)
                c_rows[g * GR : (g + 1) * GR, at] = rows[:, h * DC : (h + 1) * DC]
        for c in chunks[i]:
            lt[0, c] = c_rows[:, pl.ds(pl.multiple_of(c * DC, DC), DC)].T

    def part(m, d, c):
        return dot(lt[(m + 1) // 2, c], hid[m, d])

    def first(m):
        for d in range(2):
            rs_send[m, d, 0] = part(m, d, chunk(d, 0)).astype(BF16)
            ring(m, d, 0).start()

    def next_step(m, d, s):
        mine = part(m, d, chunk(d, s))
        ring(m, d, s - 1).wait_recv()
        rs_send[m, d, s] = (mine + rs_recv[m, d, s - 1].astype(F32)).astype(BF16)
        ring(m, d, s).start()

    def down_step(s):
        def body(d, _):
            next_step(0, d, s)
            return 0

        lax.fori_loop(0, 2, body, 0)

    def rounds(start, end):
        def body(i, _):
            m = (i // 2) % 3
            next_step(m, i % 2, 1 + i // 6 + 3 * ((2 - m) // 2))
            return 0

        lax.fori_loop(6 * start, 6 * end, body, 0)

    def late_rounds(start, end):
        def body(i, _):
            next_step(1 + (i // 2) % 2, i % 2, 1 + i // 4)
            return 0

        lax.fori_loop(4 * start, 4 * end, body, 0)

    over_peers(lambda o: a2a_piece(0, o).wait_recv())
    own(1).wait()
    take_cot(0)
    first(0)
    over_peers(lambda o: a2a_piece(2, o).start())

    def whole(m):
        return jnp.concatenate([hid[m, 0], hid[m, 1]], axis=1)

    def stack_rows(q, rows):
        for g in range(NG):
            stack[g, q] = rows[g * GR : (g + 1) * GR].astype(BF16)

    for q in range(NQ):
        stack_rows(q, dot_t(whole(0), wd[q * QW : (q + 1) * QW, :]))
    for g in range(NG):
        shuffle_out(2, g, lambda q: stack[g, q])

    over_peers(lambda o: a2a_piece(1, o).wait_recv())
    take_cot(1)
    down_step(1)
    for j in range(ND):
        lt[1, j] = x_rows[:, j * DC : (j + 1) * DC].T
    over_peers(lambda o: a2a_piece(2, o).wait_recv())
    take_cot(2)
    take_cot(3)
    over_peers(lambda o: a2a(2, o).start())
    own(2).start()
    down_step(2)

    for n in range(FF // TILE):
        cols = slice(n * TILE, (n + 1) * TILE)
        back = dot(c_rows[...], wd[:, cols])
        put_hidden(2, n, (back * fac[0, :, cols]).astype(BF16))
        put_hidden(1, n, (back * fac[1, :, cols]).astype(BF16))
    first(1)
    first(2)
    down_step(3)

    for q in range(NQ):
        rows = slice(q * QW, (q + 1) * QW)
        stack_rows(q, dot_t(whole(1), wg[rows, :]) + dot_t(whole(2), wu[rows, :]))
    for g in range(NG):
        shuffle_out(3, g, lambda q: stack[g, q])
    over_peers(lambda o: a2a(3, o).start())
    own(3).start()

    rounds(0, 2)
    over_peers(lambda o: a2a(2, o).wait_recv())
    own(2).wait()
    unshuffle_all(2)
    for q in range(NQ):
        cols = slice(q * QW, (q + 1) * QW)
        tokens_out[0, :, cols] = (dot(comb[0], x_rows[:, cols]) + dot(comb[1], x_rows[:, cols])).astype(BF16)
    stores = [pltpu.make_async_copy(tokens_out.at[0], lo_hbm, osem.at[0])]
    stores[0].start()

    rounds(2, 3)
    over_peers(lambda o: a2a(3, o).wait_recv())
    own(3).wait()
    unshuffle_all(3)
    for q in range(NQ):
        cols = slice(q * QW, (q + 1) * QW)
        tokens_out[1, :, cols] = dot(comb[2], x_rows[:, cols]).astype(BF16)
    stores.append(pltpu.make_async_copy(tokens_out.at[1], gi_hbm, osem.at[1]))
    stores[1].start()

    def finish(m, out):
        for d in range(2):
            mine = part(m, d, z)
            ring(m, d, ND - 2).wait_recv()
            total = mine + rs_recv[m, d, ND - 2].astype(F32)
            grads_out[m, :, d * HALF : (d + 1) * HALF] = total.astype(BF16)
        stores.append(pltpu.make_async_copy(grads_out.at[m], out, osem.at[2 + m]))
        stores[-1].start()

    late_rounds(3, 4)
    finish(0, gd_hbm)
    late_rounds(4, 6)
    for p in (2, 3):
        over_peers(lambda o: a2a(p, o).wait_send())
    for t in range(NP):
        over_peers(lambda o: a2a_piece(t, o).wait_send())
    finish(1, gg_hbm)
    finish(2, gu_hbm)

    def drain(i, _):
        ring((i // 2) % 3, i % 2, i // 6).wait_send()
        return 0

    lax.fori_loop(0, 6 * (ND - 1), drain, 0)
    for store in stores:
        store.wait()


def place(*refs):
    ins, outs, held, (in_sem, out_sem) = refs[:5], refs[5:10], refs[10:15], refs[15:]
    loads = [pltpu.make_async_copy(ins[i], held[i], in_sem.at[i]) for i in range(5)]
    stores = [
        pltpu.make_async_copy(held[i], outs[i] if i < 2 else outs[i].at[0], out_sem.at[i]) for i in range(5)
    ]
    for load in loads:
        load.start()
    for load, store in zip(loads, stores):
        load.wait()
        store.start()
    for store in stores:
        store.wait()


def shards(activations, expert_ids, route_gates, gate_proj, up_proj, down_proj, cotangent):
    vmem = pl.BlockSpec(memory_space=pltpu.VMEM)
    anywhere = pl.BlockSpec(memory_space=pl.ANY)
    dma = pltpu.SemaphoreType.DMA
    tokens = jax.ShapeDtypeStruct((TOK, D), BF16)
    grads = jax.ShapeDtypeStruct((DC, FF), BF16)
    out = pl.pallas_call(
        kernel,
        out_shape=(tokens,) * 2 + (grads,) * 3,
        in_specs=[vmem] * 2 + [anywhere] * 7,
        out_specs=(anywhere,) * 5,
        scratch_shapes=[
            pltpu.VMEM((TOK, D), BF16),
            pltpu.VMEM((TOK, D), BF16),
            pltpu.VMEM((D, FF), BF16),
            pltpu.VMEM((D, FF), BF16),
            pltpu.VMEM((D, FF), BF16),
            pltpu.VMEM((NP, GROUP * PIECE, 2 * GR), BF16),
            pltpu.VMEM((NP, 2 * GR, GROUP * PIECE), BF16),
            pltpu.VMEM((SLOTS, TOK), BF16),
            pltpu.VMEM((SLOTS, 1), F32),
            pltpu.VMEM((3, TOK, SLOTS), BF16),
            pltpu.VMEM((4, NE, NP, PIECE, QW), BF16),
            pltpu.VMEM((4, NE, NP, PIECE, QW), BF16),
            pltpu.VMEM((NG, NQ, GR, QW), BF16),
            pltpu.VMEM((SLOTS, D), BF16),
            pltpu.VMEM((SLOTS, D), BF16),
            pltpu.VMEM((2, ND, DC, SLOTS), BF16),
            pltpu.VMEM((2, SLOTS, FF), F32),
            pltpu.VMEM((3, 2, SLOTS, HALF), BF16),
            pltpu.VMEM((3, 2, ND - 1, DC, HALF), BF16),
            pltpu.VMEM((3, 2, ND - 1, DC, HALF), BF16),
            pltpu.VMEM((2, TOK, D), BF16),
            pltpu.VMEM((3, DC, FF), BF16),
            dma((7,)),
            dma((5,)),
            dma((4,)),
            dma((4, NE)),
            dma((4, NE)),
            dma((NP, NE)),
            dma((NP, NE)),
            dma((3, 2, ND - 1)),
            dma((3, 2, ND - 1)),
        ],
        compiler_params=pltpu.CompilerParams(
            collective_id=0, has_side_effects=True, vmem_limit_bytes=60 * 2**20
        ),
        cost_estimate=pl.CostEstimate(flops=12 * 10**9, bytes_accessed=15 * 10**6, transcendentals=300000),
        name="expert_layer",
    )(expert_ids.T, route_gates.T, activations, cotangent, gate_proj, up_proj, down_proj, *constants())
    kept = jax.ShapeDtypeStruct((1, DC, FF), BF16)
    return pl.pallas_call(
        place,
        out_shape=(tokens,) * 2 + (kept,) * 3,
        in_specs=[anywhere] * 5,
        out_specs=(anywhere,) * 5,
        scratch_shapes=[pltpu.VMEM(s.shape, BF16) for s in (tokens,) * 2 + (grads,) * 3] + [dma((5,)), dma((5,))],
        name="place",
    )(*out)


def solution(mesh):
    in_specs = (
        P(("dp", "expert"), None),
        P(("dp", "expert"), None),
        P(("dp", "expert"), None),
        P("expert", None, None),
        P("expert", None, None),
        P("expert", None, None),
        P(("dp", "expert"), None),
    )
    out_specs = (
        P(("dp", "expert"), None),
        P(("dp", "expert"), None),
        P("expert", "dp", None),
        P("expert", "dp", None),
        P("expert", "dp", None),
    )
    return jax.shard_map(shards, mesh=mesh, in_specs=in_specs, out_specs=out_specs, check_vma=False)
```

time: 164 us -> 150 us (0.915)
  local copies, waits for them, and re-layouts: 9.93 us -> 0 us
  Pallas kernels: 154 us -> 149 us
    unnamed x11 -> x0, local copies, waits for them, and re-layouts: 9.93 us -> none
    pallas_call x1 -> x2, Pallas kernels: 154 us -> 149 us  [the longest x1 146 us: shards(): pl.pallas_call(kernel, out_shape=(tokens,) * 2 + (grads,) * 3, in_specs=[...]
where the time goes in v2:
time: 150 us; the launch traced here: 149 us
  Pallas kernels  149 us (99%)
    pallas_call x1, Pallas kernels, shards(): pl.pallas_call(kernel, out_shape=(tokens,) * 2 + (grads,) * 3, in_specs=[...  146 us

profile of v2, /device:TPU:1, one launch (start us, length us, event | category | flops | bytes accessed | tf_op | source)
XLA Modules:
  0.0 149.4 jit_solution(13245533071081921114)
XLA Ops:
  0.6 146.2 %expert_layer.1 = (bf16[128,2048]{1,0:T(8,128)(2,1)}, bf16[128,2048]{1,0:T(8,128)(2,1)}, bf16[256,768]{1,0:T(8,128)(2,1)}, bf16[256,768]{1,0:T(8,128)(2,1)}, bf16[256,768]{1,0:T(8,128)(2,1)}) custom-call(s32[8,128]{1,0:T(8,128)} %bitcast.2, f32[8,128]{1,0:T(8,128)} %bitcast.3, bf16[128,2048]{1,0:T(8,128)(2,1)} %act_hbm.1, bf16[128,2048]{1,0:T(8,128)(2,1)} %cot_hbm.1, ...), custom_call_target="tpu_custom_call" | custom-call | flops 12000000000 | bytes 15000000 | tf_op jit(solution)/shard_map/expert_layer/pallas_call | solution.py:404
  146.8 2.5 %place.1 = (bf16[128,2048]{1,0:T(8,128)(2,1)}, bf16[128,2048]{1,0:T(8,128)(2,1)}, bf16[1,256,768]{2,1,0:T(8,128)(2,1)}, bf16[1,256,768]{2,1,0:T(8,128)(2,1)}, bf16[1,256,768]{2,1,0:T(8,128)(2,1)}) custom-call(bf16[128,2048]{1,0:T(8,128)(2,1)} %get-tuple-element.10.refs_0_, bf16[128,2048]{1,0:T(8,128)(2,1)} %get-tuple-element.11.refs_1_, ...), custom_call_target="tpu_custom_call" | custom-call | tf_op jit(solution)/shard_map/place/pallas_call | solution.py:449

commit v3 on v2

v3 whole, which is shorter than its diff:
```python
import functools

import jax
import jax.numpy as jnp
import numpy as np
from jax import lax
from jax.experimental import pallas as pl
from jax.experimental.pallas import tpu as pltpu
from jax.sharding import PartitionSpec as P

MESH = pl.DeviceIdType.MESH
BF16 = jnp.bfloat16
F32 = jnp.float32

CAP = 12
NE = 32
ND = 8
TOK = 128
TOP = 8
D = 2048
FF = 768
SLOTS = NE * CAP
GROUP = 8
NG = NE // GROUP
NQ = 4
QW = D // NQ
GR = GROUP * CAP
PIECE = 16
NP = CAP * NQ // PIECE
STAGES = ((0, 1), (1, 3), (3, 6))
OFFSETS = (4, 3, -3, 2, -2, 1, -1, 0)
LINKS = ND - 1
DC = D // ND
HALF = FF // 2
TILE = 256


def dot(a, b):
    return jnp.dot(a, b, preferred_element_type=F32)


def dot_t(a, b):
    return lax.dot_general(a, b, (((1,), (1,)), ((), ())), preferred_element_type=F32)


def constants():
    table = np.zeros((NP, GROUP * PIECE, 2 * GR), np.float32)
    for p in range(NP):
        for s in range(GROUP):
            for u in range(PIECE):
                q, r = divmod(p * PIECE + u, CAP)
                table[p, s * PIECE + u, (q - p) * GR + s * CAP + r] = 1.0
    return jnp.asarray(table, BF16), jnp.asarray(table.transpose(0, 2, 1), BF16)


def kernel(
    ids_hbm, gates_hbm, act_hbm, cot_hbm, wg_hbm, wu_hbm, wd_hbm, to_hbm, from_hbm,
    lo_ref, gi_ref, gg_ref, gu_ref, gd_ref,
    ids_ref, gates_ref, act, cot, wg, wu, wd, to_piece, from_piece, pick, sgate, comb, send, recv, c_send, c_recv, stack, x_rows, c_rows,
    lt, fac, hid, rs_send, rs_recv,
    wsem, lsem, ssem, rsem, csem, crem, zs, zr,
):
    me = lax.axis_index("expert")
    z = lax.axis_index("dp")
    my_y, my_x, my_c = me // 8, (me // 2) % 4, me % 2

    def peer(o):
        return (((my_y + o // 8) % 4) * 4 + (my_x + (o // 2) % 4) % 4) * 2 + (my_c + o % 2) % 2

    sources = (
        (ids_hbm, ids_ref), (gates_hbm, gates_ref), (act_hbm, act), (to_hbm, to_piece), (cot_hbm, cot),
        (from_hbm, from_piece), (wg_hbm.at[0], wg), (wu_hbm.at[0], wu), (wd_hbm.at[0], wd),
    )
    loads = [pltpu.make_async_copy(a, b, wsem.at[i]) for i, (a, b) in enumerate(sources)]
    for load in loads[:4]:
        load.start()

    barrier = pltpu.get_barrier_semaphore()

    def greet(o, _):
        pl.semaphore_signal(barrier, inc=1, device_id={"expert": peer(o)}, device_id_type=MESH)
        return 0

    lax.fori_loop(1, NE, greet, 0)
    for step in (1, ND - 1):
        pl.semaphore_signal(barrier, inc=1, device_id={"dp": (z + step) % ND}, device_id_type=MESH)
    for load in loads[4:]:
        load.start()

    def over_peers(f):
        def body(i, _):
            f((i + 20) % NE)
            return 0

        lax.fori_loop(0, 12, body, 0)
        lax.fori_loop(13, NE, body, 0)

    def a2a(p, o):
        to = peer(o)
        return pltpu.make_async_remote_copy(
            src_ref=send.at[p, to],
            dst_ref=recv.at[p, me],
            send_sem=ssem.at[p, o],
            recv_sem=rsem.at[p, o],
            device_id={"expert": to},
            device_id_type=MESH,
        )

    def a2a_cot(t, o):
        to = peer(o)
        start, end = STAGES[t]
        pieces = pl.ds(start, end - start)
        return pltpu.make_async_remote_copy(
            src_ref=c_send.at[to, pieces],
            dst_ref=c_recv.at[me, pieces],
            send_sem=csem.at[t, o],
            recv_sem=crem.at[t, o],
            device_id={"expert": to},
            device_id_type=MESH,
        )

    def own(p):
        return pltpu.make_async_copy(send.at[p, me], recv.at[p, me], lsem.at[p])

    own_cot = pltpu.make_async_copy(c_send.at[me], c_recv.at[me], lsem.at[3])

    def link(m, d, i):
        return pltpu.make_async_remote_copy(
            src_ref=rs_send.at[m, d, i],
            dst_ref=rs_recv.at[m, d, i],
            send_sem=zs.at[m, d, i],
            recv_sem=zr.at[m, d, i],
            device_id={"dp": (z + 1 - 2 * d + ND) % ND},
            device_id_type=MESH,
        )

    chunks = [(z + off + ND) % ND for off in OFFSETS]

    loads[0].wait()
    loads[1].wait()
    ids = ids_ref[...]
    gates = gates_ref[...]
    experts = lax.broadcasted_iota(jnp.int32, (NE, TOK), 0)
    named = jnp.zeros((NE, TOK), F32)
    gate_of = jnp.zeros((NE, TOK), F32)
    for k in range(TOP):
        hit = ids[k : k + 1, :] == experts
        named = named + jnp.where(hit, 1.0, 0.0)
        gate_of = gate_of + jnp.where(hit, gates[k : k + 1, :], 0.0)
    before = lax.broadcasted_iota(jnp.int32, (TOK, TOK), 0) < lax.broadcasted_iota(jnp.int32, (TOK, TOK), 1)
    earlier = dot(named.astype(BF16), jnp.where(before, 1.0, 0.0).astype(BF16))
    slot_of = jnp.where(named > 0.0, earlier, -1.0).astype(BF16)
    slots = lax.broadcasted_iota(jnp.int32, (SLOTS, NE), 0)
    first_slot = lax.broadcasted_iota(jnp.int32, (SLOTS, NE), 1) * CAP
    expand = jnp.where((slots >= first_slot) & (slots < first_slot + CAP), 1.0, 0.0)
    row = jnp.sum(expand * (slots - first_slot).astype(F32), axis=1, keepdims=True)
    expand = expand.astype(BF16)
    match = dot(expand, slot_of) == row
    high = gate_of.astype(BF16)
    rest = gate_of - high.astype(F32)
    mid = rest.astype(BF16)
    low = (rest - mid.astype(F32)).astype(BF16)
    ones = jnp.where(match, 1.0, 0.0)
    pick[...] = ones.astype(BF16)

    def shuffle_out(p, g, block):
        for t in range(NP):
            both = jnp.concatenate([block(t), block(t + 1)], axis=0)
            packed = dot(to_piece[t], both).astype(BF16)
            send[p, g * GROUP : (g + 1) * GROUP, t] = packed.reshape(GROUP, PIECE, QW)

    def unshuffle(p, q):
        out = []
        for g in range(NG):
            def piece(t):
                return recv[p, g * GROUP : (g + 1) * GROUP, t].reshape(GROUP * PIECE, QW)

            total = None
            if q < NP:
                total = dot(from_piece[q, :GR, :], piece(q))
            if q > 0:
                more = dot(from_piece[q - 1, GR:, :], piece(q - 1))
                total = more if total is None else total + more
            out.append(total.astype(BF16))
        return out

    def unshuffle_all(p):
        for q in range(NQ):
            for g, rows in enumerate(unshuffle(p, q)):
                x_rows[g * GR : (g + 1) * GR, q * QW : (q + 1) * QW] = rows

    loads[2].wait()
    loads[3].wait()
    for g in range(NG):
        rows = dot(pick[g * GR : (g + 1) * GR, :], act[...]).astype(BF16)
        shuffle_out(0, g, lambda q: rows[:, q * QW : (q + 1) * QW])
    pl.semaphore_wait(barrier, NE - 1 + 2)
    over_peers(lambda o: a2a(0, o).start())
    own(0).start()

    spread = dot(expand, high) + dot(expand, mid) + dot(expand, low)
    weight = jnp.where(match, spread, 0.0)
    sgate[...] = jnp.sum(weight, axis=1, keepdims=True)
    weight_t = weight.T
    weight_high = weight_t.astype(BF16)
    comb[0] = weight_high
    comb[1] = (weight_t - weight_high.astype(F32)).astype(BF16)
    comb[2] = ones.T.astype(BF16)

    loads[4].wait()
    for g in range(NG):
        picked, gate = pick[g * GR : (g + 1) * GR, :], sgate[g * GR : (g + 1) * GR, :]
        blocks = [
            (dot(picked, cot[:, pl.ds(pl.multiple_of(c * DC, DC), DC)]) * gate).astype(BF16) for c in chunks
        ]
        for p in range(2 * NP):
            q = p + p // NP
            both = jnp.concatenate([blocks[q], blocks[q + 1]], axis=0)
            packed = dot(to_piece[p % NP], both).astype(BF16)
            c_send[g * GROUP : (g + 1) * GROUP, p] = packed.reshape(GROUP, PIECE, DC)
    own_cot.start()

    def next_cot(o):
        a2a(0, o).wait_send()
        a2a_cot(0, o).start()

    over_peers(next_cot)
    over_peers(lambda o: a2a_cot(1, o).start())

    for load in loads[5:]:
        load.wait()
    over_peers(lambda o: a2a(0, o).wait_recv())
    own(0).wait()
    unshuffle_all(0)
    over_peers(lambda o: a2a_cot(2, o).start())

    def put_hidden(m, n, value):
        for at in range(n * TILE, (n + 1) * TILE, 128):
            d, col = at // HALF, at % HALF
            hid[m, d, :, col : col + 128] = value[:, at - n * TILE : at - n * TILE + 128]

    for n in range(FF // TILE):
        cols = slice(n * TILE, (n + 1) * TILE)
        gate_pre = dot(x_rows[...], wg[:, cols])
        up_pre = dot(x_rows[...], wu[:, cols])
        sig = 1.0 / (1.0 + jnp.exp(-gate_pre))
        silu = gate_pre * sig
        fac[0, :, cols] = silu
        fac[1, :, cols] = up_pre * sig * (1.0 + gate_pre * (1.0 - sig))
        put_hidden(0, n, (silu * up_pre).astype(BF16))

    def take_cot(q):
        at = pl.ds(pl.multiple_of(chunks[q] * DC, DC), DC)
        base, i = NP * (q // NQ), q % NQ
        for g in range(NG):
            def piece(p):
                return c_recv[g * GROUP : (g + 1) * GROUP, p].reshape(GROUP * PIECE, DC)

            total = None
            if i < NP:
                total = dot(from_piece[i, :GR, :], piece(base + i))
            if i > 0:
                more = dot(from_piece[i - 1, GR:, :], piece(base + i - 1))
                total = more if total is None else total + more
            c_rows[g * GR : (g + 1) * GR, at] = total.astype(BF16)
        lt[0, chunks[q]] = c_rows[:, at].T

    def part(m, h, c):
        return dot(lt[(m + 1) // 2, c], hid[m, h])

    def chunk(d, i):
        return (z + (1 - 2 * d) * (4 - (i + 1) // 2) + ND) % ND

    def first(m, d, i):
        rs_send[m, d, i] = part(m, (d + i) % 2, chunk(d, i)).astype(BF16)
        link(m, d, i).start()

    def then(m, d, i):
        mine = part(m, (d + i) % 2, chunk(d, i))
        link(m, d, i - 2).wait_recv()
        rs_send[m, d, i] = (mine + rs_recv[m, d, i - 2].astype(F32)).astype(BF16)
        link(m, d, i).start()

    def begin(lowest, count, i):
        def body(j, _):
            first(lowest + j // 2, j % 2, i)
            return 0

        lax.fori_loop(0, 2 * count, body, 0)

    def both_ways(m, i):
        def body(d, _):
            then(m, d, i)
            return 0

        lax.fori_loop(0, 2, body, 0)

    def rounds(start, end):
        def body(j, _):
            m = (j // 2) % 3
            then(m, j % 2, 2 + j // 6 + 2 * ((2 - m) // 2))
            return 0

        lax.fori_loop(6 * start, 6 * end, body, 0)

    def late_rounds(start, end):
        def body(j, _):
            then(1 + (j // 2) % 2, j % 2, 2 + j // 4)
            return 0

        lax.fori_loop(4 * start, 4 * end, body, 0)

    over_peers(lambda o: a2a_cot(0, o).wait_recv())
    own_cot.wait()
    take_cot(0)
    begin(0, 1, 0)

    def whole(m):
        return jnp.concatenate([hid[m, 0], hid[m, 1]], axis=1)

    def stack_rows(q, rows):
        for g in range(NG):
            stack[g, q] = rows[g * GR : (g + 1) * GR].astype(BF16)

    for q in range(NQ):
        stack_rows(q, dot_t(whole(0), wd[q * QW : (q + 1) * QW, :]))
    for g in range(NG):
        shuffle_out(1, g, lambda q: stack[g, q])

    for j in range(ND):
        lt[1, j] = x_rows[:, j * DC : (j + 1) * DC].T
    over_peers(lambda o: a2a_cot(1, o).wait_recv())
    for q in (1, 2):
        take_cot(q)
    begin(0, 1, 1)
    take_cot(3)
    both_ways(0, 2)
    over_peers(lambda o: a2a_cot(2, o).wait_recv())
    for q in (4, 5, 6, 7):
        take_cot(q)
    over_peers(lambda o: a2a(1, o).start())
    own(1).start()
    both_ways(0, 3)

    for n in range(FF // TILE):
        cols = slice(n * TILE, (n + 1) * TILE)
        back = dot(c_rows[...], wd[:, cols])
        put_hidden(2, n, (back * fac[0, :, cols]).astype(BF16))
        put_hidden(1, n, (back * fac[1, :, cols]).astype(BF16))
    begin(1, 2, 0)
    begin(1, 2, 1)

    for q in range(NQ):
        rows = slice(q * QW, (q + 1) * QW)
        stack_rows(q, dot_t(whole(1), wg[rows, :]) + dot_t(whole(2), wu[rows, :]))
    for g in range(NG):
        shuffle_out(2, g, lambda q: stack[g, q])
    over_peers(lambda o: a2a(2, o).start())
    own(2).start()

    rounds(0, 2)
    over_peers(lambda o: a2a(1, o).wait_recv())
    own(1).wait()
    unshuffle_all(1)
    for q in range(NQ):
        cols = slice(q * QW, (q + 1) * QW)
        lo_ref[:, cols] = (dot(comb[0], x_rows[:, cols]) + dot(comb[1], x_rows[:, cols])).astype(BF16)

    rounds(2, 3)
    over_peers(lambda o: a2a(2, o).wait_recv())
    own(2).wait()
    unshuffle_all(2)
    for q in range(NQ):
        cols = slice(q * QW, (q + 1) * QW)
        gi_ref[:, cols] = dot(comb[2], x_rows[:, cols]).astype(BF16)

    def finish(m, out):
        for h in range(2):
            mine = part(m, h, z)
            link(m, 1 - h, LINKS - 2).wait_recv()
            mine = mine + rs_recv[m, 1 - h, LINKS - 2].astype(F32)
            link(m, h, LINKS - 1).wait_recv()
            total = mine + rs_recv[m, h, LINKS - 1].astype(F32)
            out[:, h * HALF : (h + 1) * HALF] = total.astype(BF16)

    late_rounds(3, 4)
    finish(0, gd_ref)
    late_rounds(4, 5)
    for p in (1, 2):
        over_peers(lambda o: a2a(p, o).wait_send())
    for t in range(len(STAGES)):
        over_peers(lambda o: a2a_cot(t, o).wait_send())
    finish(1, gg_ref)
    finish(2, gu_ref)

    def drain(i, _):
        link((i // 2) % 3, i % 2, i // 6).wait_send()
        return 0

    lax.fori_loop(0, 6 * LINKS, drain, 0)


def place(*refs):
    ins, outs, sem = refs[:5], refs[5:10], refs[10]
    stores = [
        pltpu.make_async_copy(ins[i], outs[i] if i < 2 else outs[i].at[0], sem.at[i]) for i in range(5)
    ]
    for store in stores:
        store.start()
    for store in stores:
        store.wait()


def shards(activations, expert_ids, route_gates, gate_proj, up_proj, down_proj, cotangent):
    vmem = pl.BlockSpec(memory_space=pltpu.VMEM)
    anywhere = pl.BlockSpec(memory_space=pl.ANY)
    dma = pltpu.SemaphoreType.DMA
    tokens = jax.ShapeDtypeStruct((TOK, D), BF16)
    grads = jax.ShapeDtypeStruct((DC, FF), BF16)
    out = pl.pallas_call(
        kernel,
        out_shape=tuple(pltpu.VMEM(s.shape, BF16) for s in (tokens,) * 2 + (grads,) * 3),
        in_specs=[anywhere] * 9,
        out_specs=(vmem,) * 5,
        scratch_shapes=[
            pltpu.VMEM((TOP, TOK), jnp.int32),
            pltpu.VMEM((TOP, TOK), F32),
            pltpu.VMEM((TOK, D), BF16),
            pltpu.VMEM((TOK, D), BF16),
            pltpu.VMEM((D, FF), BF16),
            pltpu.VMEM((D, FF), BF16),
            pltpu.VMEM((D, FF), BF16),
            pltpu.VMEM((NP, GROUP * PIECE, 2 * GR), BF16),
            pltpu.VMEM((NP, 2 * GR, GROUP * PIECE), BF16),
            pltpu.VMEM((SLOTS, TOK), BF16),
            pltpu.VMEM((SLOTS, 1), F32),
            pltpu.VMEM((3, TOK, SLOTS), BF16),
            pltpu.VMEM((3, NE, NP, PIECE, QW), BF16),
            pltpu.VMEM((3, NE, NP, PIECE, QW), BF16),
            pltpu.VMEM((NE, 2 * NP, PIECE, DC), BF16),
            pltpu.VMEM((NE, 2 * NP, PIECE, DC), BF16),
            pltpu.VMEM((NG, NQ, GR, QW), BF16),
            pltpu.VMEM((SLOTS, D), BF16),
            pltpu.VMEM((SLOTS, D), BF16),
            pltpu.VMEM((2, ND, DC, SLOTS), BF16),
            pltpu.VMEM((2, SLOTS, FF), F32),
            pltpu.VMEM((3, 2, SLOTS, HALF), BF16),
            pltpu.VMEM((3, 2, LINKS, DC, HALF), BF16),
            pltpu.VMEM((3, 2, LINKS, DC, HALF), BF16),
            dma((9,)),
            dma((4,)),
            dma((3, NE)),
            dma((3, NE)),
            dma((len(STAGES), NE)),
            dma((len(STAGES), NE)),
            dma((3, 2, LINKS)),
            dma((3, 2, LINKS)),
        ],
        compiler_params=pltpu.CompilerParams(
            collective_id=0, has_side_effects=True, vmem_limit_bytes=54 * 2**20
        ),
        cost_estimate=pl.CostEstimate(flops=12 * 10**9, bytes_accessed=15 * 10**6, transcendentals=300000),
        name="expert_layer",
    )(expert_ids.T, route_gates.T, activations, cotangent, gate_proj, up_proj, down_proj, *constants())
    kept = jax.ShapeDtypeStruct((1, DC, FF), BF16)
    return pl.pallas_call(
        place,
        out_shape=(tokens,) * 2 + (kept,) * 3,
        in_specs=[vmem] * 5,
        out_specs=(anywhere,) * 5,
        scratch_shapes=[dma((5,))],
        compiler_params=pltpu.CompilerParams(vmem_limit_bytes=2**20),
        name="place",
    )(*out)


def solution(mesh):
    in_specs = (
        P(("dp", "expert"), None),
        P(("dp", "expert"), None),
        P(("dp", "expert"), None),
        P("expert", None, None),
        P("expert", None, None),
        P("expert", None, None),
        P(("dp", "expert"), None),
    )
    out_specs = (
        P(("dp", "expert"), None),
        P(("dp", "expert"), None),
        P("expert", "dp", None),
        P("expert", "dp", None),
        P("expert", "dp", None),
    )
    return jax.shard_map(shards, mesh=mesh, in_specs=in_specs, out_specs=out_specs, check_vma=False)
```

time: 150 us -> 142 us (0.947)
  Pallas kernels: 149 us -> 140 us
    pallas_call x2, Pallas kernels: 149 us -> 140 us  [the longest x1 139 us: shards(): pl.pallas_call(kernel, out_shape=tuple((pltpu.VMEM(s.shape, BF16) for s i...]
where the time goes in v3:
time: 142 us; the launch traced here: 141 us
  Pallas kernels  140 us (99%)
    pallas_call x1, Pallas kernels, shards(): pl.pallas_call(kernel, out_shape=tuple((pltpu.VMEM(s.shape, BF16) for s i...  139 us

profile of v3, /device:TPU:1, one launch (start us, length us, event | category | flops | bytes accessed | tf_op | source)
XLA Modules:
  0.0 141.0 jit_solution(5601459633467895718)
XLA Ops:
  0.6 138.8 %expert_layer.1 = (bf16[128,2048]{1,0:T(8,128)(2,1)S(1)}, bf16[128,2048]{1,0:T(8,128)(2,1)S(1)}, bf16[256,768]{1,0:T(8,128)(2,1)S(1)}, bf16[256,768]{1,0:T(8,128)(2,1)S(1)}, bf16[256,768]{1,0:T(8,128)(2,1)S(1)}) custom-call(s32[8,128]{1,0:T(8,128)} %bitcast.2, f32[8,128]{1,0:T(8,128)} %bitcast.3, bf16[128,2048]{1,0:T(8,128)(2,1)} %act_hbm.1, ...), custom_call_target="tpu_custom_call" | custom-call | flops 12000000000 | bytes 15000000 | tf_op jit(solution)/shard_map/expert_layer/pallas_call | solution.py:420
  139.5 1.4 place.1

commit v4 on v3

--- a/solution.py
+++ b/solution.py
@@ -27,6 +27,7 @@
 GR = GROUP * CAP
 PIECE = 16
 NP = CAP * NQ // PIECE
+FIRST = 20
 STAGES = ((0, 1), (1, 3), (3, 6))
 OFFSETS = (4, 3, -3, 2, -2, 1, -1, 0)
 LINKS = ND - 1
@@ -87,52 +88,79 @@
     for load in loads[4:]:
         load.start()
 
+    def far_peers(f):
+        def body(i, _):
+            f(i + FIRST)
+            return 0
+
+        lax.fori_loop(0, NE - FIRST, body, 0)
+
+    def near_peers(f):
+        def body(i, _):
+            f(i)
+            return 0
+
+        lax.fori_loop(1, FIRST, body, 0)
+
     def over_peers(f):
-        def body(i, _):
-            f((i + 20) % NE)
-            return 0
-
-        lax.fori_loop(0, 12, body, 0)
-        lax.fori_loop(13, NE, body, 0)
-
-    def a2a(p, o):
-        to = peer(o)
+        far_peers(f)
+        near_peers(f)
+
+    def exchange(p, to, source, held, ssem):
         return pltpu.make_async_remote_copy(
-            src_ref=send.at[p, to],
-            dst_ref=recv.at[p, me],
-            send_sem=ssem.at[p, o],
-            recv_sem=rsem.at[p, o],
+            src_ref=send.at[p, source],
+            dst_ref=recv.at[p, held],
+            send_sem=ssem,
+            recv_sem=rsem.at[p],
             device_id={"expert": to},
             device_id_type=MESH,
         )
 
-    def a2a_cot(t, o):
+    def a2a(p, o, group=0):
         to = peer(o)
+        return exchange(p, to, to, me, ssem.at[p, group])
+
+    def all_of(p, count=NE - 1, group=0):
+        some = pl.ds(0, count)
+        return exchange(p, peer(1), some, some, ssem.at[p, group])
+
+    def cot_blocks(t, to, source, held):
         start, end = STAGES[t]
         pieces = pl.ds(start, end - start)
         return pltpu.make_async_remote_copy(
-            src_ref=c_send.at[to, pieces],
-            dst_ref=c_recv.at[me, pieces],
-            send_sem=csem.at[t, o],
-            recv_sem=crem.at[t, o],
+            src_ref=c_send.at[source, pieces],
+            dst_ref=c_recv.at[held, pieces],
+            send_sem=csem.at[t],
+            recv_sem=crem.at[t],
             device_id={"expert": to},
             device_id_type=MESH,
         )
 
+    def a2a_cot(t, o):
+        to = peer(o)
+        return cot_blocks(t, to, to, me)
+
+    def all_of_cot(t):
+        some = pl.ds(0, NE - 1)
+        return cot_blocks(t, peer(1), some, some)
+
     def own(p):
         return pltpu.make_async_copy(send.at[p, me], recv.at[p, me], lsem.at[p])
 
     own_cot = pltpu.make_async_copy(c_send.at[me], c_recv.at[me], lsem.at[3])
 
-    def link(m, d, i):
+    def links(source, held, sem, d):
         return pltpu.make_async_remote_copy(
-            src_ref=rs_send.at[m, d, i],
-            dst_ref=rs_recv.at[m, d, i],
-            send_sem=zs.at[m, d, i],
-            recv_sem=zr.at[m, d, i],
+            src_ref=source,
+            dst_ref=held,
+            send_sem=zs,
+            recv_sem=sem,
             device_id={"dp": (z + 1 - 2 * d + ND) % ND},
             device_id_type=MESH,
         )
+
+    def link(m, d, i):
+        return links(rs_send.at[m, d, i], rs_recv.at[m, d, i], zr.at[m, d, i], d)
 
     chunks = [(z + off + ND) % ND for off in OFFSETS]
 
@@ -195,7 +223,8 @@
         rows = dot(pick[g * GR : (g + 1) * GR, :], act[...]).astype(BF16)
         shuffle_out(0, g, lambda q: rows[:, q * QW : (q + 1) * QW])
     pl.semaphore_wait(barrier, NE - 1 + 2)
-    over_peers(lambda o: a2a(0, o).start())
+    far_peers(lambda o: a2a(0, o, 0).start())
+    near_peers(lambda o: a2a(0, o, 1).start())
     own(0).start()
 
     spread = dot(expand, high) + dot(expand, mid) + dot(expand, low)
@@ -220,16 +249,15 @@
             c_send[g * GROUP : (g + 1) * GROUP, p] = packed.reshape(GROUP, PIECE, DC)
     own_cot.start()
 
-    def next_cot(o):
-        a2a(0, o).wait_send()
-        a2a_cot(0, o).start()
-
-    over_peers(next_cot)
+    all_of(0, NE - FIRST, 0).wait_send()
+    far_peers(lambda o: a2a_cot(0, o).start())
+    all_of(0, FIRST - 1, 1).wait_send()
+    near_peers(lambda o: a2a_cot(0, o).start())
     over_peers(lambda o: a2a_cot(1, o).start())
 
     for load in loads[5:]:
         load.wait()
-    over_peers(lambda o: a2a(0, o).wait_recv())
+    all_of(0).wait_recv()
     own(0).wait()
     unshuffle_all(0)
     over_peers(lambda o: a2a_cot(2, o).start())
@@ -310,7 +338,7 @@
 
         lax.fori_loop(4 * start, 4 * end, body, 0)
 
-    over_peers(lambda o: a2a_cot(0, o).wait_recv())
+    all_of_cot(0).wait_recv()
     own_cot.wait()
     take_cot(0)
     begin(0, 1, 0)
@@ -329,13 +357,13 @@
 
     for j in range(ND):
         lt[1, j] = x_rows[:, j * DC : (j + 1) * DC].T
-    over_peers(lambda o: a2a_cot(1, o).wait_recv())
+    all_of_cot(1).wait_recv()
     for q in (1, 2):
         take_cot(q)
     begin(0, 1, 1)
     take_cot(3)
     both_ways(0, 2)
-    over_peers(lambda o: a2a_cot(2, o).wait_recv())
+    all_of_cot(2).wait_recv()
     for q in (4, 5, 6, 7):
         take_cot(q)
     over_peers(lambda o: a2a(1, o).start())
@@ -359,7 +387,7 @@
     own(2).start()
 
     rounds(0, 2)
-    over_peers(lambda o: a2a(1, o).wait_recv())
+    all_of(1).wait_recv()
     own(1).wait()
     unshuffle_all(1)
     for q in range(NQ):
@@ -367,7 +395,7 @@
         lo_ref[:, cols] = (dot(comb[0], x_rows[:, cols]) + dot(comb[1], x_rows[:, cols])).astype(BF16)
 
     rounds(2, 3)
-    over_peers(lambda o: a2a(2, o).wait_recv())
+    all_of(2).wait_recv()
     own(2).wait()
     unshuffle_all(2)
     for q in range(NQ):
@@ -387,17 +415,13 @@
     finish(0, gd_ref)
     late_rounds(4, 5)
     for p in (1, 2):
-        over_peers(lambda o: a2a(p, o).wait_send())
+        all_of(p).wait_send()
     for t in range(len(STAGES)):
-        over_peers(lambda o: a2a_cot(t, o).wait_send())
+        all_of_cot(t).wait_send()
     finish(1, gg_ref)
     finish(2, gu_ref)
 
-    def drain(i, _):
-        link((i // 2) % 3, i % 2, i // 6).wait_send()
-        return 0
-
-    lax.fori_loop(0, 6 * LINKS, drain, 0)
+    links(rs_send, rs_recv, zr.at[0, 0, 0], 0).wait_send()
 
 
 def place(*refs):
@@ -449,11 +473,11 @@
             pltpu.VMEM((3, 2, LINKS, DC, HALF), BF16),
             dma((9,)),
             dma((4,)),
-            dma((3, NE)),
-            dma((3, NE)),
-            dma((len(STAGES), NE)),
-            dma((len(STAGES), NE)),
-            dma((3, 2, LINKS)),
+            dma((3, 2)),
+            dma((3,)),
+            dma((len(STAGES),)),
+            dma((len(STAGES),)),
+            dma,
             dma((3, 2, LINKS)),
         ],
         compiler_params=pltpu.CompilerParams(

time: 142 us -> 136 us (0.958)
  Pallas kernels: 140 us -> 135 us
    pallas_call x1, Pallas kernels: 139 us -> 134 us  [shards(): pl.pallas_call(kernel, out_shape=tuple((pltpu.VMEM(s.shape, BF16) for s i...]
where the time goes in v4:
time: 136 us
  Pallas kernels  135 us (99%)
    pallas_call x1, Pallas kernels, shards(): pl.pallas_call(kernel, out_shape=tuple((pltpu.VMEM(s.shape, BF16) for s i...  134 us

profile of v4, /device:TPU:1, one launch (start us, length us, event | category | flops | bytes accessed | tf_op | source)
XLA Modules:
  0.0 136.3 jit_solution(6675947047635773783)
XLA Ops:
  0.6 134.1 %expert_layer.1 = (bf16[128,2048]{1,0:T(8,128)(2,1)S(1)}, bf16[128,2048]{1,0:T(8,128)(2,1)S(1)}, bf16[256,768]{1,0:T(8,128)(2,1)S(1)}, bf16[256,768]{1,0:T(8,128)(2,1)S(1)}, bf16[256,768]{1,0:T(8,128)(2,1)S(1)}) custom-call(s32[8,128]{1,0:T(8,128)} %bitcast.2, f32[8,128]{1,0:T(8,128)} %bitcast.3, bf16[128,2048]{1,0:T(8,128)(2,1)} %act_hbm.1, ...), custom_call_target="tpu_custom_call" | custom-call | flops 12000000000 | bytes 15000000 | tf_op jit(solution)/shard_map/expert_layer/pallas_call | solution.py:444
  134.7 1.4 %place.1 = (bf16[128,2048]{1,0:T(8,128)(2,1)}, bf16[128,2048]{1,0:T(8,128)(2,1)}, bf16[1,256,768]{2,1,0:T(8,128)(2,1)}, bf16[1,256,768]{2,1,0:T(8,128)(2,1)}, bf16[1,256,768]{2,1,0:T(8,128)(2,1)}) custom-call(bf16[128,2048]{1,0:T(8,128)(2,1)S(1)} %get-tuple-element.10.refs_0_, bf16[128,2048]{1,0:T(8,128)(2,1)S(1)} %get-tuple-element.11.refs_1_, ...), custom_call_target="tpu_custom_call" | custom-call | tf_op jit(solution)/shard_map/place/pallas_call | solution.py:490

commit v5 on v4

--- a/solution.py
+++ b/solution.py
@@ -27,7 +27,7 @@
 GR = GROUP * CAP
 PIECE = 16
 NP = CAP * NQ // PIECE
-FIRST = 20
+ORDER = sorted(range(1, NE), key=lambda o: (-abs(2 - abs(2 - o // 8)) - abs(2 - abs(2 - o // 2 % 4)), 2 - abs(2 - o // 8), o % 2, o))
 STAGES = ((0, 1), (1, 3), (3, 6))
 OFFSETS = (4, 3, -3, 2, -2, 1, -1, 0)
 LINKS = ND - 1
@@ -88,41 +88,37 @@
     for load in loads[4:]:
         load.start()
 
-    def far_peers(f):
-        def body(i, _):
-            f(i + FIRST)
-            return 0
-
-        lax.fori_loop(0, NE - FIRST, body, 0)
-
-    def near_peers(f):
-        def body(i, _):
-            f(i)
-            return 0
-
-        lax.fori_loop(1, FIRST, body, 0)
-
     def over_peers(f):
-        far_peers(f)
-        near_peers(f)
-
-    def exchange(p, to, source, held, ssem):
+        for n, o in enumerate(ORDER):
+            f(n, o)
+
+    def mirror(o):
+        return ((4 - o // 8) % 4 * 4 + (4 - o // 2 % 4) % 4) * 2 + o % 2
+
+    def exchange(p, to, source, held, sem):
         return pltpu.make_async_remote_copy(
             src_ref=send.at[p, source],
             dst_ref=recv.at[p, held],
-            send_sem=ssem,
-            recv_sem=rsem.at[p],
+            send_sem=ssem.at[p],
+            recv_sem=rsem.at[sem],
             device_id={"expert": to},
             device_id_type=MESH,
         )
 
-    def a2a(p, o, group=0):
+    def dispatch(n, o):
         to = peer(o)
-        return exchange(p, to, to, me, ssem.at[p, group])
-
-    def all_of(p, count=NE - 1, group=0):
-        some = pl.ds(0, count)
-        return exchange(p, peer(1), some, some, ssem.at[p, group])
+        return exchange(0, to, to, n, n // GROUP)
+
+    def arrived(g):
+        count = GROUP if g < NG - 1 else GROUP - 1
+        return exchange(0, peer(1), pl.ds(0, count), pl.ds(g * GROUP, count), g)
+
+    def send_back(p, n, o):
+        return exchange(p, peer(mirror(o)), n, me, NG - 1 + p)
+
+    def all_of(p):
+        some = pl.ds(0, NE - 1)
+        return exchange(p, peer(1), some, some, NG - 1 + p)
 
     def cot_blocks(t, to, source, held):
         start, end = STAGES[t]
@@ -136,18 +132,19 @@
             device_id_type=MESH,
         )
 
-    def a2a_cot(t, o):
+    def dispatch_cot(t, n, o):
         to = peer(o)
-        return cot_blocks(t, to, to, me)
+        return cot_blocks(t, to, to, n)
 
     def all_of_cot(t):
         some = pl.ds(0, NE - 1)
         return cot_blocks(t, peer(1), some, some)
 
     def own(p):
-        return pltpu.make_async_copy(send.at[p, me], recv.at[p, me], lsem.at[p])
-
-    own_cot = pltpu.make_async_copy(c_send.at[me], c_recv.at[me], lsem.at[3])
+        source, held = (me, NE - 1) if p == 0 else (NE - 1, me)
+        return pltpu.make_async_copy(send.at[p, source], recv.at[p, held], lsem.at[p])
+
+    own_cot = pltpu.make_async_copy(c_send.at[me], c_recv.at[NE - 1], lsem.at[3])
 
     def links(source, held, sem, d):
         return pltpu.make_async_remote_copy(
@@ -197,25 +194,18 @@
             packed = dot(to_piece[t], both).astype(BF16)
             send[p, g * GROUP : (g + 1) * GROUP, t] = packed.reshape(GROUP, PIECE, QW)
 
-    def unshuffle(p, q):
-        out = []
-        for g in range(NG):
-            def piece(t):
-                return recv[p, g * GROUP : (g + 1) * GROUP, t].reshape(GROUP * PIECE, QW)
-
+    def unshuffle(p, g):
+        def piece(t):
+            return recv[p, g * GROUP : (g + 1) * GROUP, t].reshape(GROUP * PIECE, QW)
+
+        for q in range(NQ):
             total = None
             if q < NP:
                 total = dot(from_piece[q, :GR, :], piece(q))
             if q > 0:
                 more = dot(from_piece[q - 1, GR:, :], piece(q - 1))
                 total = more if total is None else total + more
-            out.append(total.astype(BF16))
-        return out
-
-    def unshuffle_all(p):
-        for q in range(NQ):
-            for g, rows in enumerate(unshuffle(p, q)):
-                x_rows[g * GR : (g + 1) * GR, q * QW : (q + 1) * QW] = rows
+            x_rows[g * GR : (g + 1) * GR, q * QW : (q + 1) * QW] = total.astype(BF16)
 
     loads[2].wait()
     loads[3].wait()
@@ -223,8 +213,7 @@
         rows = dot(pick[g * GR : (g + 1) * GR, :], act[...]).astype(BF16)
         shuffle_out(0, g, lambda q: rows[:, q * QW : (q + 1) * QW])
     pl.semaphore_wait(barrier, NE - 1 + 2)
-    far_peers(lambda o: a2a(0, o, 0).start())
-    near_peers(lambda o: a2a(0, o, 1).start())
+    over_peers(lambda n, o: dispatch(n, o).start())
     own(0).start()
 
     spread = dot(expand, high) + dot(expand, mid) + dot(expand, low)
@@ -249,33 +238,34 @@
             c_send[g * GROUP : (g + 1) * GROUP, p] = packed.reshape(GROUP, PIECE, DC)
     own_cot.start()
 
-    all_of(0, NE - FIRST, 0).wait_send()
-    far_peers(lambda o: a2a_cot(0, o).start())
-    all_of(0, FIRST - 1, 1).wait_send()
-    near_peers(lambda o: a2a_cot(0, o).start())
-    over_peers(lambda o: a2a_cot(1, o).start())
+    for t in (0, 1):
+        over_peers(lambda n, o: dispatch_cot(t, n, o).start())
 
     for load in loads[5:]:
         load.wait()
-    all_of(0).wait_recv()
-    own(0).wait()
-    unshuffle_all(0)
-    over_peers(lambda o: a2a_cot(2, o).start())
-
-    def put_hidden(m, n, value):
+    def put_hidden(m, n, value, rows=slice(0, SLOTS)):
         for at in range(n * TILE, (n + 1) * TILE, 128):
             d, col = at // HALF, at % HALF
-            hid[m, d, :, col : col + 128] = value[:, at - n * TILE : at - n * TILE + 128]
-
-    for n in range(FF // TILE):
-        cols = slice(n * TILE, (n + 1) * TILE)
-        gate_pre = dot(x_rows[...], wg[:, cols])
-        up_pre = dot(x_rows[...], wu[:, cols])
-        sig = 1.0 / (1.0 + jnp.exp(-gate_pre))
-        silu = gate_pre * sig
-        fac[0, :, cols] = silu
-        fac[1, :, cols] = up_pre * sig * (1.0 + gate_pre * (1.0 - sig))
-        put_hidden(0, n, (silu * up_pre).astype(BF16))
+            hid[m, d, rows, col : col + 128] = value[:, at - n * TILE : at - n * TILE + 128]
+
+    for half in range(2):
+        for g in (2 * half, 2 * half + 1):
+            arrived(g).wait_recv()
+            if g == NG - 1:
+                own(0).wait()
+            unshuffle(0, g)
+        if half == 1:
+            over_peers(lambda n, o: dispatch_cot(2, n, o).start())
+        rows = slice(half * SLOTS // 2, (half + 1) * SLOTS // 2)
+        for n in range(FF // TILE):
+            cols = slice(n * TILE, (n + 1) * TILE)
+            gate_pre = dot(x_rows[rows, :], wg[:, cols])
+            up_pre = dot(x_rows[rows, :], wu[:, cols])
+            sig = 1.0 / (1.0 + jnp.exp(-gate_pre))
+            silu = gate_pre * sig
+            fac[0, rows, cols] = silu
+            fac[1, rows, cols] = up_pre * sig * (1.0 + gate_pre * (1.0 - sig))
+            put_hidden(0, n, (silu * up_pre).astype(BF16), rows)
 
     def take_cot(q):
         at = pl.ds(pl.multiple_of(chunks[q] * DC, DC), DC)
@@ -366,7 +356,7 @@
     all_of_cot(2).wait_recv()
     for q in (4, 5, 6, 7):
         take_cot(q)
-    over_peers(lambda o: a2a(1, o).start())
+    over_peers(lambda n, o: send_back(1, n, o).start())
     own(1).start()
     both_ways(0, 3)
 
@@ -383,13 +373,14 @@
         stack_rows(q, dot_t(whole(1), wg[rows, :]) + dot_t(whole(2), wu[rows, :]))
     for g in range(NG):
         shuffle_out(2, g, lambda q: stack[g, q])
-    over_peers(lambda o: a2a(2, o).start())
+    over_peers(lambda n, o: send_back(2, n, o).start())
     own(2).start()
 
     rounds(0, 2)
     all_of(1).wait_recv()
     own(1).wait()
-    unshuffle_all(1)
+    for g in range(NG):
+        unshuffle(1, g)
     for q in range(NQ):
         cols = slice(q * QW, (q + 1) * QW)
         lo_ref[:, cols] = (dot(comb[0], x_rows[:, cols]) + dot(comb[1], x_rows[:, cols])).astype(BF16)
@@ -397,7 +388,8 @@
     rounds(2, 3)
     all_of(2).wait_recv()
     own(2).wait()
-    unshuffle_all(2)
+    for g in range(NG):
+        unshuffle(2, g)
     for q in range(NQ):
         cols = slice(q * QW, (q + 1) * QW)
         gi_ref[:, cols] = dot(comb[2], x_rows[:, cols]).astype(BF16)
@@ -414,7 +406,7 @@
     late_rounds(3, 4)
     finish(0, gd_ref)
     late_rounds(4, 5)
-    for p in (1, 2):
+    for p in range(3):
         all_of(p).wait_send()
     for t in range(len(STAGES)):
         all_of_cot(t).wait_send()
@@ -473,8 +465,8 @@
             pltpu.VMEM((3, 2, LINKS, DC, HALF), BF16),
             dma((9,)),
             dma((4,)),
-            dma((3, 2)),
             dma((3,)),
+            dma((NG + 2,)),
             dma((len(STAGES),)),
             dma((len(STAGES),)),
             dma,

time: 136 us -> 130 us (0.956)
  Pallas kernels: 135 us -> 129 us
    pallas_call x1, Pallas kernels: 134 us -> 128 us  [shards(): pl.pallas_call(kernel, out_shape=tuple((pltpu.VMEM(s.shape, BF16) for s i...]
where the time goes in v5:
time: 130 us
  Pallas kernels  129 us (99%)
    pallas_call x1, Pallas kernels, shards(): pl.pallas_call(kernel, out_shape=tuple((pltpu.VMEM(s.shape, BF16) for s i...  128 us

profile of v5, /device:TPU:1, one launch (start us, length us, event | category | flops | bytes accessed | tf_op | source)
XLA Modules:
  0.0 130.1 jit_solution(1939223748194566791)
XLA Ops:
  0.6 127.9 %expert_layer.1 = (bf16[128,2048]{1,0:T(8,128)(2,1)S(1)}, bf16[128,2048]{1,0:T(8,128)(2,1)S(1)}, bf16[256,768]{1,0:T(8,128)(2,1)S(1)}, bf16[256,768]{1,0:T(8,128)(2,1)S(1)}, bf16[256,768]{1,0:T(8,128)(2,1)S(1)}) custom-call(s32[8,128]{1,0:T(8,128)} %bitcast.2, f32[8,128]{1,0:T(8,128)} %bitcast.3, bf16[128,2048]{1,0:T(8,128)(2,1)} %act_hbm.1, ...), custom_call_target="tpu_custom_call" | custom-call | flops 12000000000 | bytes 15000000 | tf_op jit(solution)/shard_map/expert_layer/pallas_call | solution.py:436
  128.5 1.4 %place.1 = (bf16[128,2048]{1,0:T(8,128)(2,1)}, bf16[128,2048]{1,0:T(8,128)(2,1)}, bf16[1,256,768]{2,1,0:T(8,128)(2,1)}, bf16[1,256,768]{2,1,0:T(8,128)(2,1)}, bf16[1,256,768]{2,1,0:T(8,128)(2,1)}) custom-call(bf16[128,2048]{1,0:T(8,128)(2,1)S(1)} %get-tuple-element.10.refs_0_, bf16[128,2048]{1,0:T(8,128)(2,1)S(1)} %get-tuple-element.11.refs_1_, ...), custom_call_target="tpu_custom_call" | custom-call | tf_op jit(solution)/shard_map/place/pallas_call | solution.py:482

commit v6 on v5

--- a/solution.py
+++ b/solution.py
@@ -27,7 +27,7 @@
 GR = GROUP * CAP
 PIECE = 16
 NP = CAP * NQ // PIECE
-ORDER = sorted(range(1, NE), key=lambda o: (-abs(2 - abs(2 - o // 8)) - abs(2 - abs(2 - o // 2 % 4)), 2 - abs(2 - o // 8), o % 2, o))
+ORDER = sorted(range(1, NE), key=lambda o: (o % 2, -abs(2 - abs(2 - o // 8)) - abs(2 - abs(2 - o // 2 % 4)), 2 - abs(2 - o // 8), o))
 STAGES = ((0, 1), (1, 3), (3, 6))
 OFFSETS = (4, 3, -3, 2, -2, 1, -1, 0)
 LINKS = ND - 1
@@ -58,7 +58,7 @@
     ids_hbm, gates_hbm, act_hbm, cot_hbm, wg_hbm, wu_hbm, wd_hbm, to_hbm, from_hbm,
     lo_ref, gi_ref, gg_ref, gu_ref, gd_ref,
     ids_ref, gates_ref, act, cot, wg, wu, wd, to_piece, from_piece, pick, sgate, comb, send, recv, c_send, c_recv, stack, x_rows, c_rows,
-    lt, fac, hid, rs_send, rs_recv,
+    lt, fac, hid, rs_send, rs_recv, met,
     wsem, lsem, ssem, rsem, csem, crem, zs, zr,
 ):
     me = lax.axis_index("expert")
@@ -249,14 +249,14 @@
             hid[m, d, rows, col : col + 128] = value[:, at - n * TILE : at - n * TILE + 128]
 
     for half in range(2):
-        for g in (2 * half, 2 * half + 1):
+        for g in ((0, 1, 2), (3,))[half]:
             arrived(g).wait_recv()
             if g == NG - 1:
                 own(0).wait()
             unshuffle(0, g)
         if half == 1:
             over_peers(lambda n, o: dispatch_cot(2, n, o).start())
-        rows = slice(half * SLOTS // 2, (half + 1) * SLOTS // 2)
+        rows = slice(half * 3 * GR, (3 + half) * GR)
         for n in range(FF // TILE):
             cols = slice(n * TILE, (n + 1) * TILE)
             gate_pre = dot(x_rows[rows, :], wg[:, cols])
@@ -394,18 +394,24 @@
         cols = slice(q * QW, (q + 1) * QW)
         gi_ref[:, cols] = dot(comb[2], x_rows[:, cols]).astype(BF16)
 
-    def finish(m, out):
+    def meet(m):
         for h in range(2):
             mine = part(m, h, z)
             link(m, 1 - h, LINKS - 2).wait_recv()
-            mine = mine + rs_recv[m, 1 - h, LINKS - 2].astype(F32)
+            met[m, h] = mine + rs_recv[m, 1 - h, LINKS - 2].astype(F32)
+
+    def finish(m, out):
+        for h in range(2):
             link(m, h, LINKS - 1).wait_recv()
-            total = mine + rs_recv[m, h, LINKS - 1].astype(F32)
+            total = met[m, h] + rs_recv[m, h, LINKS - 1].astype(F32)
             out[:, h * HALF : (h + 1) * HALF] = total.astype(BF16)
 
     late_rounds(3, 4)
+    meet(0)
     finish(0, gd_ref)
     late_rounds(4, 5)
+    meet(1)
+    meet(2)
     for p in range(3):
         all_of(p).wait_send()
     for t in range(len(STAGES)):
@@ -418,9 +424,13 @@
 
 def place(*refs):
     ins, outs, sem = refs[:5], refs[5:10], refs[10]
-    stores = [
-        pltpu.make_async_copy(ins[i], outs[i] if i < 2 else outs[i].at[0], sem.at[i]) for i in range(5)
-    ]
+    stores = []
+    for i in range(5):
+        rows = ins[i].shape[0] // 2
+        for h in range(2):
+            some = pl.ds(h * rows, rows)
+            out = outs[i].at[some] if i < 2 else outs[i].at[0, some]
+            stores.append(pltpu.make_async_copy(ins[i].at[some], out, sem.at[2 * i + h]))
     for store in stores:
         store.start()
     for store in stores:
@@ -463,6 +473,7 @@
             pltpu.VMEM((3, 2, SLOTS, HALF), BF16),
             pltpu.VMEM((3, 2, LINKS, DC, HALF), BF16),
             pltpu.VMEM((3, 2, LINKS, DC, HALF), BF16),
+            pltpu.VMEM((3, 2, DC, HALF), F32),
             dma((9,)),
             dma((4,)),
             dma((3,)),
@@ -484,7 +495,7 @@
         out_shape=(tokens,) * 2 + (kept,) * 3,
         in_specs=[vmem] * 5,
         out_specs=(anywhere,) * 5,
-        scratch_shapes=[dma((5,))],
+        scratch_shapes=[dma((10,))],
         compiler_params=pltpu.CompilerParams(vmem_limit_bytes=2**20),
         name="place",
     )(*out)

time: 130 us -> 130 us (level)
  no operation moved by 1% of the time
where the time goes in v6:
time: 130 us
  Pallas kernels  129 us (99%)
    pallas_call x1, Pallas kernels, shards(): pl.pallas_call(kernel, out_shape=tuple((pltpu.VMEM(s.shape, BF16) for s i...  127 us

profile of v6, /device:TPU:1, one launch (start us, length us, event | category | flops | bytes accessed | tf_op | source)
XLA Modules:
  0.0 129.6 jit_solution(13218793025950117447)
XLA Ops:
  0.6 127.4 %expert_layer.1 = (bf16[128,2048]{1,0:T(8,128)(2,1)S(1)}, bf16[128,2048]{1,0:T(8,128)(2,1)S(1)}, bf16[256,768]{1,0:T(8,128)(2,1)S(1)}, bf16[256,768]{1,0:T(8,128)(2,1)S(1)}, bf16[256,768]{1,0:T(8,128)(2,1)S(1)}) custom-call(s32[8,128]{1,0:T(8,128)} %bitcast.2, f32[8,128]{1,0:T(8,128)} %bitcast.3, bf16[128,2048]{1,0:T(8,128)(2,1)} %act_hbm.1, ...), custom_call_target="tpu_custom_call" | custom-call | flops 12000000000 | bytes 15000000 | tf_op jit(solution)/shard_map/expert_layer/pallas_call | solution.py:446
  128.0 1.4 %place.1 = (bf16[128,2048]{1,0:T(8,128)(2,1)}, bf16[128,2048]{1,0:T(8,128)(2,1)}, bf16[1,256,768]{2,1,0:T(8,128)(2,1)}, bf16[1,256,768]{2,1,0:T(8,128)(2,1)}, bf16[1,256,768]{2,1,0:T(8,128)(2,1)}) custom-call(bf16[128,2048]{1,0:T(8,128)(2,1)S(1)} %get-tuple-element.10.refs_0_, bf16[128,2048]{1,0:T(8,128)(2,1)S(1)} %get-tuple-element.11.refs_1_, ...), custom_call_target="tpu_custom_call" | custom-call | tf_op jit(solution)/shard_map/place/pallas_call | solution.py:493

commit v7 on v6

--- a/solution.py
+++ b/solution.py
@@ -156,8 +156,12 @@
             device_id_type=MESH,
         )
 
-    def link(m, d, i):
-        return links(rs_send.at[m, d, i], rs_recv.at[m, d, i], zr.at[m, d, i], d)
+    def link(kind, d, i):
+        some = pl.ds(kind, 1 + kind)
+        return links(rs_send.at[d, i, some], rs_recv.at[d, i, some], zr.at[kind, d, i], d)
+
+    def members(kind):
+        return (1, 2) if kind else (0,)
 
     chunks = [(z + off + ND) % ND for off in OFFSETS]
 
@@ -289,49 +293,51 @@
     def chunk(d, i):
         return (z + (1 - 2 * d) * (4 - (i + 1) // 2) + ND) % ND
 
-    def first(m, d, i):
-        rs_send[m, d, i] = part(m, (d + i) % 2, chunk(d, i)).astype(BF16)
-        link(m, d, i).start()
-
-    def then(m, d, i):
-        mine = part(m, (d + i) % 2, chunk(d, i))
-        link(m, d, i - 2).wait_recv()
-        rs_send[m, d, i] = (mine + rs_recv[m, d, i - 2].astype(F32)).astype(BF16)
-        link(m, d, i).start()
-
-    def begin(lowest, count, i):
-        def body(j, _):
-            first(lowest + j // 2, j % 2, i)
+    def first(kind, d, i):
+        for m in members(kind):
+            rs_send[d, i, m] = part(m, (d + i) % 2, chunk(d, i)).astype(BF16)
+        link(kind, d, i).start()
+
+    def then(kind, d, i):
+        link(kind, d, i - 2).wait_recv()
+        for m in members(kind):
+            mine = part(m, (d + i) % 2, chunk(d, i))
+            rs_send[d, i, m] = (mine + rs_recv[d, i - 2, m].astype(F32)).astype(BF16)
+        link(kind, d, i).start()
+
+    def begin(kind, i):
+        def body(d, _):
+            first(kind, d, i)
             return 0
 
-        lax.fori_loop(0, 2 * count, body, 0)
-
-    def both_ways(m, i):
+        lax.fori_loop(0, 2, body, 0)
+
+    def both_ways(kind, i):
         def body(d, _):
-            then(m, d, i)
+            then(kind, d, i)
             return 0
 
         lax.fori_loop(0, 2, body, 0)
 
     def rounds(start, end):
         def body(j, _):
-            m = (j // 2) % 3
-            then(m, j % 2, 2 + j // 6 + 2 * ((2 - m) // 2))
+            then(0, j % 2, 4 + j // 2)
+            then(1, j % 2, 2 + j // 2)
             return 0
 
-        lax.fori_loop(6 * start, 6 * end, body, 0)
+        lax.fori_loop(2 * start, 2 * end, body, 0)
 
     def late_rounds(start, end):
         def body(j, _):
-            then(1 + (j // 2) % 2, j % 2, 2 + j // 4)
+            then(1, j % 2, 2 + j // 2)
             return 0
 
-        lax.fori_loop(4 * start, 4 * end, body, 0)
+        lax.fori_loop(2 * start, 2 * end, body, 0)
 
     all_of_cot(0).wait_recv()
     own_cot.wait()
     take_cot(0)
-    begin(0, 1, 0)
+    begin(0, 0)
 
     def whole(m):
         return jnp.concatenate([hid[m, 0], hid[m, 1]], axis=1)
@@ -350,7 +356,7 @@
     all_of_cot(1).wait_recv()
     for q in (1, 2):
         take_cot(q)
-    begin(0, 1, 1)
+    begin(0, 1)
     take_cot(3)
     both_ways(0, 2)
     all_of_cot(2).wait_recv()
@@ -365,8 +371,8 @@
         back = dot(c_rows[...], wd[:, cols])
         put_hidden(2, n, (back * fac[0, :, cols]).astype(BF16))
         put_hidden(1, n, (back * fac[1, :, cols]).astype(BF16))
-    begin(1, 2, 0)
-    begin(1, 2, 1)
+    begin(1, 0)
+    begin(1, 1)
 
     for q in range(NQ):
         rows = slice(q * QW, (q + 1) * QW)
@@ -394,30 +400,29 @@
         cols = slice(q * QW, (q + 1) * QW)
         gi_ref[:, cols] = dot(comb[2], x_rows[:, cols]).astype(BF16)
 
-    def meet(m):
+    def meet(kind):
         for h in range(2):
-            mine = part(m, h, z)
-            link(m, 1 - h, LINKS - 2).wait_recv()
-            met[m, h] = mine + rs_recv[m, 1 - h, LINKS - 2].astype(F32)
-
-    def finish(m, out):
+            link(kind, 1 - h, LINKS - 2).wait_recv()
+            for m in members(kind):
+                met[m % 2, h] = part(m, h, z) + rs_recv[1 - h, LINKS - 2, m].astype(F32)
+
+    def finish(kind):
         for h in range(2):
-            link(m, h, LINKS - 1).wait_recv()
-            total = met[m, h] + rs_recv[m, h, LINKS - 1].astype(F32)
-            out[:, h * HALF : (h + 1) * HALF] = total.astype(BF16)
+            link(kind, h, LINKS - 1).wait_recv()
+            for m in members(kind):
+                total = met[m % 2, h] + rs_recv[h, LINKS - 1, m].astype(F32)
+                (gd_ref, gg_ref, gu_ref)[m][:, h * HALF : (h + 1) * HALF] = total.astype(BF16)
 
     late_rounds(3, 4)
     meet(0)
-    finish(0, gd_ref)
+    finish(0)
     late_rounds(4, 5)
     meet(1)
-    meet(2)
     for p in range(3):
         all_of(p).wait_send()
     for t in range(len(STAGES)):
         all_of_cot(t).wait_send()
-    finish(1, gg_ref)
-    finish(2, gu_ref)
+    finish(1)
 
     links(rs_send, rs_recv, zr.at[0, 0, 0], 0).wait_send()
 
@@ -471,9 +476,9 @@
             pltpu.VMEM((2, ND, DC, SLOTS), BF16),
             pltpu.VMEM((2, SLOTS, FF), F32),
             pltpu.VMEM((3, 2, SLOTS, HALF), BF16),
-            pltpu.VMEM((3, 2, LINKS, DC, HALF), BF16),
-            pltpu.VMEM((3, 2, LINKS, DC, HALF), BF16),
-            pltpu.VMEM((3, 2, DC, HALF), F32),
+            pltpu.VMEM((2, LINKS, 3, DC, HALF), BF16),
+            pltpu.VMEM((2, LINKS, 3, DC, HALF), BF16),
+            pltpu.VMEM((2, 2, DC, HALF), F32),
             dma((9,)),
             dma((4,)),
             dma((3,)),
@@ -481,10 +486,10 @@
             dma((len(STAGES),)),
             dma((len(STAGES),)),
             dma,
-            dma((3, 2, LINKS)),
+            dma((2, 2, LINKS)),
         ],
         compiler_params=pltpu.CompilerParams(
-            collective_id=0, has_side_effects=True, vmem_limit_bytes=54 * 2**20
+            collective_id=0, has_side_effects=True, vmem_limit_bytes=57 * 2**20
         ),
         cost_estimate=pl.CostEstimate(flops=12 * 10**9, bytes_accessed=15 * 10**6, transcendentals=300000),
         name="expert_layer",

time: 130 us -> 130 us (level)
  no operation moved by 1% of the time
where the time goes in v7:
time: 130 us
  Pallas kernels  129 us (99%)
    pallas_call x1, Pallas kernels, shards(): pl.pallas_call(kernel, out_shape=tuple((pltpu.VMEM(s.shape, BF16) for s i...  127 us

profile of v7, /device:TPU:1, one launch (start us, length us, event | category | flops | bytes accessed | tf_op | source)
XLA Modules:
  0.0 129.6 jit_solution(5907908725865591718)
XLA Ops:
  0.6 127.4 %expert_layer.1 = (bf16[128,2048]{1,0:T(8,128)(2,1)S(1)}, bf16[128,2048]{1,0:T(8,128)(2,1)S(1)}, bf16[256,768]{1,0:T(8,128)(2,1)S(1)}, bf16[256,768]{1,0:T(8,128)(2,1)S(1)}, bf16[256,768]{1,0:T(8,128)(2,1)S(1)}) custom-call(s32[8,128]{1,0:T(8,128)} %bitcast.2, f32[8,128]{1,0:T(8,128)} %bitcast.3, bf16[128,2048]{1,0:T(8,128)(2,1)} %act_hbm.1, ...), custom_call_target="tpu_custom_call" | custom-call | flops 12000000000 | bytes 15000000 | tf_op jit(solution)/shard_map/expert_layer/pallas_call | solution.py:451
  128.0 1.4 %place.1 = (bf16[128,2048]{1,0:T(8,128)(2,1)}, bf16[128,2048]{1,0:T(8,128)(2,1)}, bf16[1,256,768]{2,1,0:T(8,128)(2,1)}, bf16[1,256,768]{2,1,0:T(8,128)(2,1)}, bf16[1,256,768]{2,1,0:T(8,128)(2,1)}) custom-call(bf16[128,2048]{1,0:T(8,128)(2,1)S(1)} %get-tuple-element.10.refs_0_, bf16[128,2048]{1,0:T(8,128)(2,1)S(1)} %get-tuple-element.11.refs_1_, ...), custom_call_target="tpu_custom_call" | custom-call | tf_op jit(solution)/shard_map/place/pallas_call | solution.py:498
